TPU v7x, 32 devices: a whole 2x2x4 slice. The times are simulated.
32 devices in a mesh: dp: 16 (over z, x, core), seq: 2 (over y).
Axes of the slice: x: 2, y: 2, z: 4, core: 2. Of those that a mesh axis runs over, the one named last changes fastest.
Arguments:
- tokens: bfloat16 [32, 1024, 1024], P('dp', 'seq'), may hold values from -6 to 6
- text_states: bfloat16 [32, 256, 1024], P('dp', 'seq'), may hold values from -6 to 6
- unit_length: int32 [32], P('dp'), may hold values from 512 to 1024, as said below
- text_length: int32 [32], P('dp'), may hold values from 64 to 256, as said below
- cotangent: bfloat16 [32, 1024, 1024], P('dp', 'seq'), may hold values from -6 to 6
- attn_gain: bfloat16 [1024], P(('dp', 'seq')), may hold values from 0.5 to 1.5
- attn_shift: bfloat16 [1024], P(('dp', 'seq')), may hold values from -1 to 1
- attn_inputs: bfloat16 [1024, 3072], P(('dp', 'seq')), may hold values from -0.1875 to 0.1875
- attn_qbias: bfloat16 [1024], P(('dp', 'seq')), may hold values from -1 to 1
- attn_vbias: bfloat16 [1024], P(('dp', 'seq')), may hold values from -1 to 1
- attn_output: bfloat16 [1024, 1024], P(('dp', 'seq')), may hold values from -0.75 to 0.75
- attn_obias: bfloat16 [1024], P(('dp', 'seq')), may hold values from -1 to 1
- cross_gain: bfloat16 [1024], P(('dp', 'seq')), may hold values from 0.5 to 1.5
- cross_shift: bfloat16 [1024], P(('dp', 'seq')), may hold values from -1 to 1
- cross_query: bfloat16 [1024, 1024], P(('dp', 'seq')), may hold values from -0.1875 to 0.1875
- cross_qbias: bfloat16 [1024], P(('dp', 'seq')), may hold values from -1 to 1
- cross_keyval: bfloat16 [1024, 2048], P(('dp', 'seq')), may hold values from -0.1875 to 0.1875
- cross_vbias: bfloat16 [1024], P(('dp', 'seq')), may hold values from -1 to 1
- cross_output: bfloat16 [1024, 1024], P(('dp', 'seq')), may hold values from -0.375 to 0.375
- cross_obias: bfloat16 [1024], P(('dp', 'seq')), may hold values from -1 to 1
- ffn_gain: bfloat16 [1024], P(('dp', 'seq')), may hold values from 0.5 to 1.5
- ffn_shift: bfloat16 [1024], P(('dp', 'seq')), may hold values from -1 to 1
- ffn_up: bfloat16 [1024, 4096], P(('dp', 'seq')), may hold values from -0.1875 to 0.1875
- ffn_upbias: bfloat16 [4096], P(('dp', 'seq')), may hold values from -1 to 1
- ffn_down: bfloat16 [4096, 1024], P(('dp', 'seq')), may hold values from -0.125 to 0.125
- ffn_downbias: bfloat16 [1024], P(('dp', 'seq')), may hold values from -1 to 1
- final_gain: bfloat16 [1024], P(('dp', 'seq')), may hold values from 0.5 to 1.5
- final_shift: bfloat16 [1024], P(('dp', 'seq')), may hold values from -1 to 1
Outputs:
- layer_out: bfloat16 [32, 1024, 1024], P('dp', 'seq')
- tokens_grad: bfloat16 [32, 1024, 1024], P('dp', 'seq')
- text_grad: bfloat16 [32, 256, 1024], P('dp', 'seq')
- grad_attn_gain: float32 [1024], P(('dp', 'seq'))
- grad_attn_shift: float32 [1024], P(('dp', 'seq'))
- grad_attn_inputs: float32 [1024, 3072], P(('dp', 'seq'))
- grad_attn_qbias: float32 [1024], P(('dp', 'seq'))
- grad_attn_vbias: float32 [1024], P(('dp', 'seq'))
- grad_attn_output: float32 [1024, 1024], P(('dp', 'seq'))
- grad_attn_obias: float32 [1024], P(('dp', 'seq'))
- grad_cross_gain: float32 [1024], P(('dp', 'seq'))
- grad_cross_shift: float32 [1024], P(('dp', 'seq'))
- grad_cross_query: float32 [1024, 1024], P(('dp', 'seq'))
- grad_cross_qbias: float32 [1024], P(('dp', 'seq'))
- grad_cross_keyval: float32 [1024, 2048], P(('dp', 'seq'))
- grad_cross_vbias: float32 [1024], P(('dp', 'seq'))
- grad_cross_output: float32 [1024, 1024], P(('dp', 'seq'))
- grad_cross_obias: float32 [1024], P(('dp', 'seq'))
- grad_ffn_gain: float32 [1024], P(('dp', 'seq'))
- grad_ffn_shift: float32 [1024], P(('dp', 'seq'))
- grad_ffn_up: float32 [1024, 4096], P(('dp', 'seq'))
- grad_ffn_upbias: float32 [4096], P(('dp', 'seq'))
- grad_ffn_down: float32 [4096, 1024], P(('dp', 'seq'))
- grad_ffn_downbias: float32 [1024], P(('dp', 'seq'))
- grad_final_gain: float32 [1024], P(('dp', 'seq'))
- grad_final_shift: float32 [1024], P(('dp', 'seq'))
Inputs may be any that keep to these rules, and one draw needn't show every extreme that they name: `unit_length`: each is 512, 768 or 1024; among the 2 sequences of each index of dp one has 1024 and another 1024//2. `text_length`: some sequence has 256 and another 256//4.
All inputs are finite; a program needn't handle non-finite values.
Results may differ from a plain program's by a relative error of at most 0.035.
Values may be sent and summed in bfloat16 or wider, within the bound.
A program may use at most 320 MiB of HBM per device.

v0:
```python
import math

import jax
import jax.numpy as jnp
from jax import lax
from jax.sharding import PartitionSpec as P

HEADS = 16
HEAD_DIM = 64


EPSILON = 1e-05
MASKED = -1e30


def layer_norm(values, norm_gain, norm_shift):
    center = values - jnp.mean(values, axis=-1, keepdims=True)
    spread = jnp.mean(center * center, axis=-1, keepdims=True)
    return center * lax.rsqrt(spread + EPSILON) * norm_gain + norm_shift


def norm_back(values, norm_gain, norm_shift, upstream):
    result, pullback = jax.vjp(layer_norm, values, norm_gain, norm_shift)
    return pullback(upstream)


def rows_dot(left_side, right_side):
    return jnp.dot(left_side, right_side, preferred_element_type=jnp.float32)


def left_dot(left_side, right_side):
    return lax.dot_general(
        left_side, right_side, (((0,), (0,)), ((), ())), preferred_element_type=jnp.float32
    )


def right_dot(left_side, right_side):
    return lax.dot_general(
        left_side, right_side, (((1,), (1,)), ((), ())), preferred_element_type=jnp.float32
    )


def heads_of(matrix):
    return matrix.reshape(matrix.shape[0], HEADS, HEAD_DIM)


def attend_forward(queries, key_rows, value_rows, allowed):
    score_scale = 1.0 / math.sqrt(HEAD_DIM)
    scores = (
        jnp.einsum(
            "qhd,khd->hqk",
            heads_of(queries),
            heads_of(key_rows),
            preferred_element_type=jnp.float32,
        )
        * score_scale
    )
    scores = jnp.where(allowed[None], scores, MASKED)
    row_max = jnp.max(scores, axis=-1, keepdims=True)
    weights = jnp.exp(scores - row_max)
    row_total = jnp.sum(weights, axis=-1, keepdims=True)
    weights = (weights / row_total).astype(jnp.bfloat16)
    mixed_rows = jnp.einsum(
        "hqk,khd->qhd", weights, heads_of(value_rows), preferred_element_type=jnp.float32
    )
    logsum = (row_max + jnp.log(row_total))[..., 0]
    return (mixed_rows.reshape(queries.shape[0], -1).astype(jnp.bfloat16), logsum)


def attend_back(queries, key_rows, value_rows, allowed, logsum, upstream):
    score_scale = 1.0 / math.sqrt(HEAD_DIM)
    query_heads = heads_of(queries)
    key_heads = heads_of(key_rows)
    upstream_heads = heads_of(upstream)
    scores = (
        jnp.einsum("qhd,khd->hqk", query_heads, key_heads, preferred_element_type=jnp.float32)
        * score_scale
    )
    scores = jnp.where(allowed[None], scores, MASKED)
    weights = jnp.exp(scores - logsum[..., None])
    grad_weights = jnp.einsum(
        "qhd,khd->hqk", upstream_heads, heads_of(value_rows), preferred_element_type=jnp.float32
    )
    row_delta = jnp.sum(weights * grad_weights, axis=-1, keepdims=True)
    grad_scores = (weights * (grad_weights - row_delta)).astype(jnp.bfloat16)
    grad_query = (
        jnp.einsum("hqk,khd->qhd", grad_scores, key_heads, preferred_element_type=jnp.float32)
        * score_scale
    )
    grad_key = (
        jnp.einsum("hqk,qhd->khd", grad_scores, query_heads, preferred_element_type=jnp.float32)
        * score_scale
    )
    grad_value = jnp.einsum(
        "hqk,qhd->khd",
        weights.astype(jnp.bfloat16),
        upstream_heads,
        preferred_element_type=jnp.float32,
    )
    key_count = key_rows.shape[0]
    return (
        grad_query.reshape(queries.shape[0], -1),
        grad_key.reshape(key_count, -1),
        grad_value.reshape(key_count, -1),
    )


def to_float(values):
    return values.astype(jnp.float32)


def on_device(
    tokens,
    text_states,
    unit_length,
    text_length,
    cotangent,
    attn_gain,
    attn_shift,
    attn_inputs,
    attn_qbias,
    attn_vbias,
    attn_output,
    attn_obias,
    cross_gain,
    cross_shift,
    cross_query,
    cross_qbias,
    cross_keyval,
    cross_vbias,
    cross_output,
    cross_obias,
    ffn_gain,
    ffn_shift,
    ffn_up,
    ffn_upbias,
    ffn_down,
    ffn_downbias,
    final_gain,
    final_shift,
):
    seq_count, local_len, model_width = tokens.shape
    row_count = seq_count * local_len
    first_pos = lax.axis_index("seq") * local_len
    zero_bias = jnp.zeros((model_width,), jnp.float32)
    (
        a_gain_full,
        a_shift_full,
        attention_input_weight_whole,
        a_qbias_full,
        a_vbias_full,
        a_output_full,
        a_obias_full,
    ) = (
        lax.all_gather(attn_gain, ("dp", "seq"), axis=0, tiled=True),
        lax.all_gather(attn_shift, ("dp", "seq"), axis=0, tiled=True),
        lax.all_gather(attn_inputs, ("dp", "seq"), axis=0, tiled=True),
        lax.all_gather(attn_qbias, ("dp", "seq"), axis=0, tiled=True),
        lax.all_gather(attn_vbias, ("dp", "seq"), axis=0, tiled=True),
        lax.all_gather(attn_output, ("dp", "seq"), axis=0, tiled=True),
        lax.all_gather(attn_obias, ("dp", "seq"), axis=0, tiled=True),
    )
    inputs = to_float(tokens).reshape(row_count, model_width)
    normed_one = layer_norm(inputs, to_float(a_gain_full), to_float(a_shift_full)).astype(
        jnp.bfloat16
    )
    joined = rows_dot(normed_one, attention_input_weight_whole) + jnp.concatenate(
        [to_float(a_qbias_full), zero_bias, to_float(a_vbias_full)]
    )
    joined = joined.astype(jnp.bfloat16)
    self_queries = joined[:, :model_width].reshape(seq_count, local_len, model_width)
    keyval_local = joined[:, model_width:].reshape(seq_count, local_len, 2 * model_width)
    self_keyval = lax.all_gather(keyval_local, "seq", axis=1, tiled=True)
    full_len = self_keyval.shape[1]
    causal = jnp.arange(full_len)[None, :] <= (first_pos + jnp.arange(local_len))[:, None]

    def self_forward(packed):
        seq_queries, seq_keyval = packed
        return attend_forward(
            seq_queries, seq_keyval[:, :model_width], seq_keyval[:, model_width:], causal
        )

    self_mixed, self_logsum = lax.map(self_forward, (self_queries, self_keyval))
    self_flat = self_mixed.reshape(row_count, model_width)
    after_self = inputs + rows_dot(self_flat, a_output_full) + to_float(a_obias_full)
    (
        c_gain_full,
        c_shift_full,
        c_query_full,
        c_qbias_full,
        c_keyval_full,
        cross_value_bias_whole,
        c_output_full,
        c_obias_full,
    ) = (
        lax.all_gather(cross_gain, ("dp", "seq"), axis=0, tiled=True),
        lax.all_gather(cross_shift, ("dp", "seq"), axis=0, tiled=True),
        lax.all_gather(cross_query, ("dp", "seq"), axis=0, tiled=True),
        lax.all_gather(cross_qbias, ("dp", "seq"), axis=0, tiled=True),
        lax.all_gather(cross_keyval, ("dp", "seq"), axis=0, tiled=True),
        lax.all_gather(cross_vbias, ("dp", "seq"), axis=0, tiled=True),
        lax.all_gather(cross_output, ("dp", "seq"), axis=0, tiled=True),
        lax.all_gather(cross_obias, ("dp", "seq"), axis=0, tiled=True),
    )
    normed_two = layer_norm(after_self, to_float(c_gain_full), to_float(c_shift_full)).astype(
        jnp.bfloat16
    )
    cross_queries = (rows_dot(normed_two, c_query_full) + to_float(c_qbias_full)).astype(
        jnp.bfloat16
    )
    cross_queries = cross_queries.reshape(seq_count, local_len, model_width)
    keyval_bias = jnp.concatenate([zero_bias, to_float(cross_value_bias_whole)])
    text_whole = lax.all_gather(text_states, "seq", axis=1, tiled=True)
    cross_kv = (rows_dot(text_whole.reshape(-1, model_width), c_keyval_full) + keyval_bias).astype(
        jnp.bfloat16
    )
    cross_kv = cross_kv.reshape(seq_count, -1, 2 * model_width)
    text_total = cross_kv.shape[1]
    text_allowed = jnp.arange(text_total)[None, :] < text_length[:, None]

    def cross_forward(packed):
        seq_queries, seq_keyval, seq_allowed = packed
        allowed = jnp.broadcast_to(seq_allowed[None, :], (local_len, text_total))
        return attend_forward(
            seq_queries, seq_keyval[:, :model_width], seq_keyval[:, model_width:], allowed
        )

    cross_blended_rows, cross_logsum = lax.map(
        cross_forward, (cross_queries, cross_kv, text_allowed)
    )
    cross_flat = cross_blended_rows.reshape(row_count, model_width)
    after_cross = after_self + rows_dot(cross_flat, c_output_full) + to_float(c_obias_full)
    (
        f_gain_full,
        feedforward_shift_whole,
        f_up_full,
        f_upbias_full,
        f_down_full,
        f_downbias_full,
        z_gain_full,
        z_shift_full,
    ) = (
        lax.all_gather(ffn_gain, ("dp", "seq"), axis=0, tiled=True),
        lax.all_gather(ffn_shift, ("dp", "seq"), axis=0, tiled=True),
        lax.all_gather(ffn_up, ("dp", "seq"), axis=0, tiled=True),
        lax.all_gather(ffn_upbias, ("dp", "seq"), axis=0, tiled=True),
        lax.all_gather(ffn_down, ("dp", "seq"), axis=0, tiled=True),
        lax.all_gather(ffn_downbias, ("dp", "seq"), axis=0, tiled=True),
        lax.all_gather(final_gain, ("dp", "seq"), axis=0, tiled=True),
        lax.all_gather(final_shift, ("dp", "seq"), axis=0, tiled=True),
    )
    normed_three = layer_norm(
        after_cross, to_float(f_gain_full), to_float(feedforward_shift_whole)
    ).astype(jnp.bfloat16)
    ffn_inner = rows_dot(normed_three, f_up_full) + to_float(f_upbias_full)
    active = jax.nn.gelu(ffn_inner).astype(jnp.bfloat16)
    after_ffn = after_cross + rows_dot(active, f_down_full) + to_float(f_downbias_full)
    valid_rows = ((first_pos + jnp.arange(local_len))[None, :] < unit_length[:, None]).astype(
        jnp.float32
    )
    valid_rows = valid_rows.reshape(row_count, 1)
    final_norm = layer_norm(after_ffn, to_float(z_gain_full), to_float(z_shift_full))
    layer_out = (
        (final_norm * valid_rows).astype(jnp.bfloat16).reshape(seq_count, local_len, model_width)
    )
    (
        f_gain_full,
        feedforward_shift_whole,
        f_up_full,
        f_upbias_full,
        f_down_full,
        f_downbias_full,
        z_gain_full,
        z_shift_full,
    ) = (
        lax.all_gather(ffn_gain, ("dp", "seq"), axis=0, tiled=True),
        lax.all_gather(ffn_shift, ("dp", "seq"), axis=0, tiled=True),
        lax.all_gather(ffn_up, ("dp", "seq"), axis=0, tiled=True),
        lax.all_gather(ffn_upbias, ("dp", "seq"), axis=0, tiled=True),
        lax.all_gather(ffn_down, ("dp", "seq"), axis=0, tiled=True),
        lax.all_gather(ffn_downbias, ("dp", "seq"), axis=0, tiled=True),
        lax.all_gather(final_gain, ("dp", "seq"), axis=0, tiled=True),
        lax.all_gather(final_shift, ("dp", "seq"), axis=0, tiled=True),
    )
    upstream = to_float(cotangent).reshape(row_count, model_width) * valid_rows
    grad_after_ffn, grad_zgain, grad_zshift = norm_back(
        after_ffn, to_float(z_gain_full), to_float(z_shift_full), upstream
    )
    grad_branch = grad_after_ffn.astype(jnp.bfloat16)
    grad_down = left_dot(active, grad_branch)
    grad_downbias = jnp.sum(to_float(grad_branch), axis=0)
    grad_active = right_dot(grad_branch, f_down_full)
    inner_value, gelu_back = jax.vjp(jax.nn.gelu, ffn_inner)
    grad_inner = gelu_back(grad_active)[0].astype(jnp.bfloat16)
    grad_up = left_dot(normed_three, grad_inner)
    grad_upbias = jnp.sum(to_float(grad_inner), axis=0)
    grad_normed_three = right_dot(grad_inner, f_up_full)
    grad_cross_norm, grad_fgain, grad_fshift = norm_back(
        after_cross, to_float(f_gain_full), to_float(feedforward_shift_whole), grad_normed_three
    )
    grad_after_cross = grad_after_ffn + grad_cross_norm
    ffn_sums = (
        lax.psum_scatter(grad_fgain, ("dp", "seq"), scatter_dimension=0, tiled=True),
        lax.psum_scatter(grad_fshift, ("dp", "seq"), scatter_dimension=0, tiled=True),
        lax.psum_scatter(grad_up, ("dp", "seq"), scatter_dimension=0, tiled=True),
        lax.psum_scatter(grad_upbias, ("dp", "seq"), scatter_dimension=0, tiled=True),
        lax.psum_scatter(grad_down, ("dp", "seq"), scatter_dimension=0, tiled=True),
        lax.psum_scatter(grad_downbias, ("dp", "seq"), scatter_dimension=0, tiled=True),
        lax.psum_scatter(grad_zgain, ("dp", "seq"), scatter_dimension=0, tiled=True),
        lax.psum_scatter(grad_zshift, ("dp", "seq"), scatter_dimension=0, tiled=True),
    )
    (
        c_gain_full,
        c_shift_full,
        c_query_full,
        c_qbias_full,
        c_keyval_full,
        cross_value_bias_whole,
        c_output_full,
        c_obias_full,
    ) = (
        lax.all_gather(cross_gain, ("dp", "seq"), axis=0, tiled=True),
        lax.all_gather(cross_shift, ("dp", "seq"), axis=0, tiled=True),
        lax.all_gather(cross_query, ("dp", "seq"), axis=0, tiled=True),
        lax.all_gather(cross_qbias, ("dp", "seq"), axis=0, tiled=True),
        lax.all_gather(cross_keyval, ("dp", "seq"), axis=0, tiled=True),
        lax.all_gather(cross_vbias, ("dp", "seq"), axis=0, tiled=True),
        lax.all_gather(cross_output, ("dp", "seq"), axis=0, tiled=True),
        lax.all_gather(cross_obias, ("dp", "seq"), axis=0, tiled=True),
    )
    cross_branch_gradient = grad_after_cross.astype(jnp.bfloat16)
    grad_coutput = left_dot(cross_flat, cross_branch_gradient)
    grad_cobias = jnp.sum(to_float(cross_branch_gradient), axis=0)
    grad_cross_mixed = right_dot(cross_branch_gradient, c_output_full).astype(jnp.bfloat16)
    grad_cross_mixed = grad_cross_mixed.reshape(seq_count, local_len, model_width)

    def cross_backward(packed):
        seq_queries, seq_keyval, seq_allowed, sequence_log_sum_exp, seq_upstream = packed
        allowed = jnp.broadcast_to(seq_allowed[None, :], (local_len, text_total))
        return attend_back(
            seq_queries,
            seq_keyval[:, :model_width],
            seq_keyval[:, model_width:],
            allowed,
            sequence_log_sum_exp,
            seq_upstream,
        )

    grad_cq, grad_ck, grad_cv = lax.map(
        cross_backward, (cross_queries, cross_kv, text_allowed, cross_logsum, grad_cross_mixed)
    )
    grad_ckv = lax.psum_scatter(
        jnp.concatenate([grad_ck, grad_cv], axis=-1).astype(jnp.bfloat16),
        "seq",
        scatter_dimension=1,
        tiled=True,
    ).astype(jnp.float32)
    grad_ckv = grad_ckv.astype(jnp.bfloat16).reshape(-1, 2 * model_width)
    grad_ckeyval = left_dot(text_states.reshape(-1, model_width), grad_ckv)
    grad_cvbias = jnp.sum(to_float(grad_ckv[:, model_width:]), axis=0)
    text_grad = right_dot(grad_ckv, c_keyval_full).astype(jnp.bfloat16).reshape(text_states.shape)
    grad_cq_low = grad_cq.reshape(row_count, model_width).astype(jnp.bfloat16)
    grad_cquery = left_dot(normed_two, grad_cq_low)
    grad_cqbias = jnp.sum(to_float(grad_cq_low), axis=0)
    grad_normed_two = right_dot(grad_cq_low, c_query_full)
    grad_self_norm, grad_cgain, grad_cshift = norm_back(
        after_self, to_float(c_gain_full), to_float(c_shift_full), grad_normed_two
    )
    grad_after_self = grad_after_cross + grad_self_norm
    cross_sums = (
        lax.psum_scatter(grad_cgain, ("dp", "seq"), scatter_dimension=0, tiled=True),
        lax.psum_scatter(grad_cshift, ("dp", "seq"), scatter_dimension=0, tiled=True),
        lax.psum_scatter(grad_cquery, ("dp", "seq"), scatter_dimension=0, tiled=True),
        lax.psum_scatter(grad_cqbias, ("dp", "seq"), scatter_dimension=0, tiled=True),
        lax.psum_scatter(grad_ckeyval, ("dp", "seq"), scatter_dimension=0, tiled=True),
        lax.psum_scatter(grad_cvbias, ("dp", "seq"), scatter_dimension=0, tiled=True),
        lax.psum_scatter(grad_coutput, ("dp", "seq"), scatter_dimension=0, tiled=True),
        lax.psum_scatter(grad_cobias, ("dp", "seq"), scatter_dimension=0, tiled=True),
    )
    (
        a_gain_full,
        a_shift_full,
        attention_input_weight_whole,
        a_qbias_full,
        a_vbias_full,
        a_output_full,
        a_obias_full,
    ) = (
        lax.all_gather(attn_gain, ("dp", "seq"), axis=0, tiled=True),
        lax.all_gather(attn_shift, ("dp", "seq"), axis=0, tiled=True),
        lax.all_gather(attn_inputs, ("dp", "seq"), axis=0, tiled=True),
        lax.all_gather(attn_qbias, ("dp", "seq"), axis=0, tiled=True),
        lax.all_gather(attn_vbias, ("dp", "seq"), axis=0, tiled=True),
        lax.all_gather(attn_output, ("dp", "seq"), axis=0, tiled=True),
        lax.all_gather(attn_obias, ("dp", "seq"), axis=0, tiled=True),
    )
    grad_self_branch = grad_after_self.astype(jnp.bfloat16)
    grad_aoutput = left_dot(self_flat, grad_self_branch)
    grad_aobias = jnp.sum(to_float(grad_self_branch), axis=0)
    grad_self_mixed = right_dot(grad_self_branch, a_output_full).astype(jnp.bfloat16)
    grad_self_mixed = grad_self_mixed.reshape(seq_count, local_len, model_width)

    def self_backward(packed):
        seq_queries, seq_keyval, sequence_log_sum_exp, seq_upstream = packed
        return attend_back(
            seq_queries,
            seq_keyval[:, :model_width],
            seq_keyval[:, model_width:],
            causal,
            sequence_log_sum_exp,
            seq_upstream,
        )

    gradient_self_query, grad_sk, grad_sv = lax.map(
        self_backward, (self_queries, self_keyval, self_logsum, grad_self_mixed)
    )
    gradient_self_keyvalue = lax.psum_scatter(
        jnp.concatenate([grad_sk, grad_sv], axis=-1).astype(jnp.bfloat16),
        "seq",
        scatter_dimension=1,
        tiled=True,
    ).astype(jnp.float32)
    grad_joined = (
        jnp.concatenate([gradient_self_query, gradient_self_keyvalue], axis=-1)
        .reshape(row_count, 3 * model_width)
        .astype(jnp.bfloat16)
    )
    grad_ainputs = left_dot(normed_one, grad_joined)
    grad_aqbias = jnp.sum(to_float(grad_joined[:, :model_width]), axis=0)
    grad_avbias = jnp.sum(to_float(grad_joined[:, 2 * model_width :]), axis=0)
    grad_normed_one = right_dot(grad_joined, attention_input_weight_whole)
    grad_input_norm, grad_again, grad_ashift = norm_back(
        inputs, to_float(a_gain_full), to_float(a_shift_full), grad_normed_one
    )
    tokens_grad = (
        (grad_after_self + grad_input_norm)
        .astype(jnp.bfloat16)
        .reshape(seq_count, local_len, model_width)
    )
    attn_sums = (
        lax.psum_scatter(grad_again, ("dp", "seq"), scatter_dimension=0, tiled=True),
        lax.psum_scatter(grad_ashift, ("dp", "seq"), scatter_dimension=0, tiled=True),
        lax.psum_scatter(grad_ainputs, ("dp", "seq"), scatter_dimension=0, tiled=True),
        lax.psum_scatter(grad_aqbias, ("dp", "seq"), scatter_dimension=0, tiled=True),
        lax.psum_scatter(grad_avbias, ("dp", "seq"), scatter_dimension=0, tiled=True),
        lax.psum_scatter(grad_aoutput, ("dp", "seq"), scatter_dimension=0, tiled=True),
        lax.psum_scatter(grad_aobias, ("dp", "seq"), scatter_dimension=0, tiled=True),
    )
    return (layer_out, tokens_grad, text_grad, *attn_sums, *cross_sums, *ffn_sums)


def solution(mesh):
    in_specs = (
        P("dp", "seq", None),
        P("dp", "seq", None),
        P("dp"),
        P("dp"),
        P("dp", "seq", None),
        P(("dp", "seq")),
        P(("dp", "seq")),
        P(("dp", "seq"), None),
        P(("dp", "seq")),
        P(("dp", "seq")),
        P(("dp", "seq"), None),
        P(("dp", "seq")),
        P(("dp", "seq")),
        P(("dp", "seq")),
        P(("dp", "seq"), None),
        P(("dp", "seq")),
        P(("dp", "seq"), None),
        P(("dp", "seq")),
        P(("dp", "seq"), None),
        P(("dp", "seq")),
        P(("dp", "seq")),
        P(("dp", "seq")),
        P(("dp", "seq"), None),
        P(("dp", "seq")),
        P(("dp", "seq"), None),
        P(("dp", "seq")),
        P(("dp", "seq")),
        P(("dp", "seq")),
    )
    out_specs = (
        P("dp", "seq", None),
        P("dp", "seq", None),
        P("dp", "seq", None),
        P(("dp", "seq")),
        P(("dp", "seq")),
        P(("dp", "seq"), None),
        P(("dp", "seq")),
        P(("dp", "seq")),
        P(("dp", "seq"), None),
        P(("dp", "seq")),
        P(("dp", "seq")),
        P(("dp", "seq")),
        P(("dp", "seq"), None),
        P(("dp", "seq")),
        P(("dp", "seq"), None),
        P(("dp", "seq")),
        P(("dp", "seq"), None),
        P(("dp", "seq")),
        P(("dp", "seq")),
        P(("dp", "seq")),
        P(("dp", "seq"), None),
        P(("dp", "seq")),
        P(("dp", "seq"), None),
        P(("dp", "seq")),
        P(("dp", "seq")),
        P(("dp", "seq")),
    )
    return jax.shard_map(
        on_device, mesh=mesh, in_specs=in_specs, out_specs=out_specs, check_vma=False
    )
```

profile of v0, /device:TPU:0, one launch (start us, length us, event | category | flops | bytes accessed | tf_op | source)
XLA Modules:
  0.0 2791.4 jit_solution(14385874695070727584)
XLA Ops:
  22.0 43.0 %all-reduce.33 = (bf16[1024]{0:T(1024)(128)(2,1)S(1)}, bf16[1024]{0:T(1024)(128)(2,1)S(1)}, bf16[1024]{0:T(1024)(128)(2,1)S(1)}, bf16[1024]{0:T(1024)(128)(2,1)S...) all-reduce(bf16[1024]{0:T(1024)(128)(2,1)S(1)} %dynamic-update-slic, ...), channel_id=1, replica_groups=mesh['dp'=16,'seq'=2] {'dp','seq'}, use_global_device_ids=true, to_apply=%add.5 | all-reduce | flops 15360 | bytes 61440
  71.8 12.1 all-gather.11.cloned.1.call-done
  83.8 9.4 add_convert_fusion
  97.2 6.2 copy.100
  114.8 65.8 %all-gather = bf16[32,1,128]{2,1,0:T(2,128)(2,1)S(1)} all-gather(bf16[1,1,128]{2,1,0:T(2,128)(2,1)S(1)} %bitcast.347), channel_id=1, replica_groups=mesh['dp'=16,'seq'=2] {'dp','seq'}, dimensions={0}, use_global_device_ids=true | all-gather | bytes 8448 | tf_op jit(solution)/shard_map/all_gather | solution.py:246
  181.3 5.5 add_convert_fusion.5
  195.3 79.0 %all-gather.13.cloned.1.call-done = bf16[2,1024,2048]{1,2,0:T(8,128)(2,1)} async-done(((bf16[2,512,2048]{1,2,0:T(8,128)(2,1)}), bf16[2,1024,2048]{1,2,0:T(8,128)(2,1)}) %all-gather.13.cloned.1.call-update) | async-done | bytes 8388624 | tf_op jit(solution)/shard_map/all_gather | solution.py:173
  275.9 101.3 %while.56 = (s32[]{:T(128)}, bf16[2,512,1024]{2,1,0:T(8,128)(2,1)}, f32[2,16,512]{2,1,0:T(8,128)S(1)}, bf16[2,1024,2048]{1,2,0:T(8,128)(2,1)}, bf16[2,512,1024]{...) while((s32[]{:T(128)}, bf16[2,512,1024]{2,1,0:T(8,128)(2,1)}, f32[2,16,512]{2,1,0:T(8,128)S(1)}, ...), condition=%wide.region_5.6_spmd.clone, body=%wide.region_2.5_spmd.clone.sunk | while | flops 2249187328 | bytes 132384864 | solution.py:183
  279.4 13.9 fusion.209
  293.4 15.0 fusion.210
  308.4 15.5 fusion.211
  330.0 14.0 fusion.209
  344.0 14.9 fusion.210
  358.9 15.3 fusion.211
  377.2 6.1 fusion.83
  386.4 5.7 all-gather.21.cloned.1.call-done
  392.2 6.6 add_convert_fusion.3
  403.3 22.7 while.54
  426.1 24.6 all-gather.23.cloned.1.call-done
  450.7 5.9 fusion.84
  459.3 70.8 %all-gather.25.cloned.1.call-done = bf16[1024,4096]{1,0:T(8,128)(2,1)} async-done(((bf16[32,4096]{1,0:T(8,128)(2,1)}), bf16[1024,4096]{1,0:T(8,128)(2,1)}) %all-gather.25.cloned.1.call-update) | async-done | bytes 8388624 | tf_op jit(solution)/shard_map/all_gather | solution.py:245
  530.1 16.7 fusion.70
  546.8 62.5 %all-gather.27.cloned.1.call-done = bf16[4096,1024]{1,0:T(8,128)(2,1)} async-done(((bf16[128,1024]{1,0:T(8,128)(2,1)}), bf16[4096,1024]{1,0:T(8,128)(2,1)}) %all-gather.27.cloned.1.call-update) | async-done | bytes 8388624 | tf_op jit(solution)/shard_map/all_gather | solution.py:247
  609.3 17.4 fusion.85
  639.1 26.4 convert_reduce_fusion
  665.6 16.4 multiply_reduce_fusion.4
  691.1 61.1 %while.55 = (s32[]{:T(128)}, bf16[2,512,1024]{2,1,0:T(8,128)(2,1)}, bf16[2,256,1024]{2,1,0:T(8,128)(2,1)}, bf16[2,256,1024]{2,1,0:T(8,128)(2,1)}, bf16[2,256,204...) while((s32[]{:T(128)}, bf16[2,512,1024]{2,1,0:T(8,128)(2,1)}, ...), condition=%wide.region_22.23_spmd, body=%wide.region_20.22_spmd.sunk | while | flops 1375199232 | bytes 173770240 | solution.py:349
  703.9 5.7 multiply_reduce_fusion.14
  734.4 5.7 multiply_reduce_fusion.14
  755.7 6.5 multiply_reduce_fusion.5
  772.4 257.3 %while.57 = (s32[]{:T(128)}, bf16[2,512,1024]{2,1,0:T(8,128)(2,1)}, bf16[2,1024,1024]{2,1,0:T(8,128)(2,1)}, bf16[2,1024,1024]{2,1,0:T(8,128)(2,1)}, bf16[2,1024,...) while((s32[]{:T(128)}, bf16[2,512,1024]{2,1,0:T(8,128)(2,1)}, ...), condition=%wide.region_27.28_spmd.clone, body=%wide.region_25.27_spmd.clone.sunk | while | flops 5498200064 | bytes 326338752 | solution.py:414
  782.3 13.1 fusion.223
  795.5 16.8 fusion.224
  816.3 26.0 multiply_reduce_fusion.15
  842.2 28.0 %multiply_convert_fusion.9 = bf16[16,512,1024]{2,1,0:T(8,128)(2,1)} fusion(f32[16,512,1024]{2,1,0:T(8,128)} %get-tuple-element.779, f32[16,512,1024]{2,1,0:T(8,128)} %fusion.223, f32[16,512]{1,0:T(8,128)S(1)} %get-tuple-element.780, f32[16,512]{1,0:T(8,128)S(1)} %dynamic-slice_bitcast_fusion.17, pred[512,1024]{1,0:T(8,128)(4,1)} %iota_compare_fusion.6), kind=kLoop, calls=%fused_computation.16.clone.1 | loop fusion | flops 50331648 | bytes 84475904 | tf_op jit(solution)/shard_map/while/body/eval_jaxpr/convert_element_type | solution.py:85
  870.2 12.0 convolution_multiply_fusion.10
  882.2 8.8 convolution_multiply_fusion.11
  910.7 13.1 fusion.223
  923.8 16.8 fusion.224
  944.6 26.0 multiply_reduce_fusion.15
  970.5 28.0 %multiply_convert_fusion.9 = bf16[16,512,1024]{2,1,0:T(8,128)(2,1)} fusion(f32[16,512,1024]{2,1,0:T(8,128)} %get-tuple-element.779, f32[16,512,1024]{2,1,0:T(8,128)} %fusion.223, f32[16,512]{1,0:T(8,128)S(1)} %get-tuple-element.780, f32[16,512]{1,0:T(8,128)S(1)} %dynamic-slice_bitcast_fusion.17, pred[512,1024]{1,0:T(8,128)(4,1)} %iota_compare_fusion.6), kind=kLoop, calls=%fused_computation.16.clone.1 | loop fusion | flops 50331648 | bytes 84475904 | tf_op jit(solution)/shard_map/while/body/eval_jaxpr/convert_element_type | solution.py:85
  998.5 12.0 convolution_multiply_fusion.10
  1010.5 8.8 convolution_multiply_fusion.11
  1029.8 8.2 pad_maximum_fusion
  1044.9 91.1 %reduce-scatter.12.cloned.1.call-done = bf16[2,512,2048]{2,1,0:T(8,128)(2,1)} async-done(((bf16[2,1024,2048]{2,1,0:T(8,128)(2,1)}), bf16[2,512,2048]{2,1,0:T(8,128)(2,1)}) %reduce-scatter.12.cloned.1.call-update) | async-done | bytes 4194320 | tf_op jit(solution)/shard_map/reduce_scatter | solution.py:417
  1140.9 9.8 fusion.73
  1155.6 7.2 fusion.63
  1163.4 7.5 fusion.71
  1171.0 6.6 fusion.88
  1178.8 5.6 convolution_bitcast_fusion.1
  1184.4 9.2 copy.126
  1194.4 20.1 fusion.72
  1215.2 16.8 fusion.69
  1232.7 12.1 convolution_bitcast_fusion
  1244.9 4.4 convolution_convert_fusion.2
  1249.3 5.4 add_convert_fusion.1
  1254.7 31.1 %all-reduce.36.cloned.1.call-done = (f32[1024]{0:T(1024)}, f32[1024]{0:T(1024)}, f32[1024]{0:T(1024)}, f32[1024]{0:T(1024)}, f32[1024]{0:T(1024)}, /*index=5*/f3...) async-done(((f32[1024]{0:T(1024)}, f32[1024]{0:T(1024)}, ...) | async-done | bytes 77840
  1306.0 128.5 %reduce-scatter.22.cloned.1.call-done = f32[32,1024]{1,0:T(8,128)} async-done(((f32[1024,1024]{1,0:T(8,128)}), f32[32,1024]{1,0:T(8,128)}) %reduce-scatter.22.cloned.1.call-update) | async-done | bytes 131088 | tf_op jit(solution)/shard_map/reduce_scatter | solution.py:377
  1434.5 141.1 %reduce-scatter.20.cloned.1.call-done = f32[32,1024]{1,0:T(8,128)} async-done(((f32[1024,1024]{1,0:T(8,128)}), f32[32,1024]{1,0:T(8,128)}) %reduce-scatter.20.cloned.1.call-update) | async-done | bytes 131088 | tf_op jit(solution)/shard_map/reduce_scatter | solution.py:373
  1575.6 141.0 %reduce-scatter.18.cloned.1.call-done = f32[32,1024]{1,0:T(8,128)} async-done(((f32[1024,1024]{1,0:T(8,128)}), f32[32,1024]{1,0:T(8,128)}) %reduce-scatter.18.cloned.1.call-update) | async-done | bytes 131088 | tf_op jit(solution)/shard_map/reduce_scatter | solution.py:446
  1716.6 182.9 %reduce-scatter.28.cloned.1.call-done = f32[32,2048]{1,0:T(8,128)} async-done(((f32[1024,2048]{1,0:T(8,128)}), f32[32,2048]{1,0:T(8,128)}) %reduce-scatter.28.cloned.1.call-update) | async-done | bytes 262160
  1899.5 360.5 %reduce-scatter.26.cloned.1.call-done = f32[128,1024]{1,0:T(8,128)} async-done(((f32[4096,1024]{1,0:T(8,128)}), f32[128,1024]{1,0:T(8,128)}) %reduce-scatter.26.cloned.1.call-update) | async-done | bytes 524304 | tf_op jit(solution)/shard_map/reduce_scatter | solution.py:307
  2260.1 361.2 %reduce-scatter.24.cloned.1.call-done = f32[32,4096]{1,0:T(8,128)} async-done(((f32[1024,4096]{1,0:T(8,128)}), f32[32,4096]{1,0:T(8,128)}) %reduce-scatter.24.cloned.1.call-update) | async-done | bytes 524304 | tf_op jit(solution)/shard_map/reduce_scatter | solution.py:305
  2621.3 163.1 %reduce-scatter.16.cloned.1.call-done = f32[32,3072]{1,0:T(8,128)} async-done(((f32[1024,3072]{1,0:T(8,128)}), f32[32,3072]{1,0:T(8,128)}) %reduce-scatter.16.cloned.1.call-update) | async-done | bytes 393232 | tf_op jit(solution)/shard_map/reduce_scatter | solution.py:443
  (434 shorter events, 264.8 us)
Async XLA Ops:
  7.2 59.9 %copy-start.7 = (bf16[2,512,1024]{2,1,0:T(8,128)(2,1)S(1)}, bf16[2,512,1024]{2,1,0:T(8,128)(2,1)}, u32[]{:S(2)}) copy-start(bf16[2,512,1024]{2,1,0:T(8,128)(2,1)} %param.36) | copy-start | bytes 6291460
  7.2 76.6 %all-gather.11.cloned.1.call-start = ((), (), s32[]{:S(2)}) async-start(), calls=%async_computation.9 | async-start | bytes 6488064 | tf_op jit(solution)/shard_map/all_gather | solution.py:157
  7.9 173.3 %all-gather.17.cloned.1.call-start = ((), (), s32[]{:S(2)}) async-start(), calls=%async_computation.12 | async-start | bytes 1572864 | tf_op jit(solution)/shard_map/all_gather | solution.py:213
  8.7 172.6 %all-gather.19.cloned.1.call-start = ((), (), s32[]{:S(2)}) async-start(), calls=%async_computation.13 | async-start | bytes 4325376 | tf_op jit(solution)/shard_map/all_gather | solution.py:200
  9.4 264.9 %all-gather.13.cloned.1.call-start = ((), (), s32[]{:S(2)}) async-start(), calls=%async_computation.10 | async-start | bytes 12582912 | tf_op jit(solution)/shard_map/all_gather | solution.py:173
  65.0 4.0 copy-start.31
  65.0 4.0 copy-start.66
  93.2 4.0 copy-start.23
  103.5 3.5 copy-start.81
  103.5 10.1 copy-start.78
  103.5 11.3 copy-start.77
  103.5 273.7 %all-gather.15.cloned.1.call-start = ((), (), s32[]{:S(2)}) async-start(), calls=%async_computation.11 | async-start | bytes 2162688 | tf_op jit(solution)/shard_map/all_gather | solution.py:160
  104.1 288.1 %all-gather.21.cloned.1.call-start = ((), (), s32[]{:S(2)}) async-start(), calls=%async_computation.14 | async-start | bytes 2162688 | tf_op jit(solution)/shard_map/all_gather | solution.py:198
  104.7 346.0 %all-gather.23.cloned.1.call-start = ((), (), s32[]{:S(2)}) async-start(), calls=%async_computation.15 | async-start | bytes 2162688 | tf_op jit(solution)/shard_map/all_gather | solution.py:202
  105.4 424.7 %all-gather.25.cloned.1.call-start = ((), (), s32[]{:S(2)}) async-start(), calls=%async_computation.16 | async-start | bytes 8650752 | tf_op jit(solution)/shard_map/all_gather | solution.py:245
  106.2 503.1 %all-gather.27.cloned.1.call-start = ((), (), s32[]{:S(2)}) async-start(), calls=%async_computation.17 | async-start | bytes 8650752 | tf_op jit(solution)/shard_map/all_gather | solution.py:247
  106.9 936.2 %reduce-scatter.14.cloned.1.call-start = ((), (), s32[]{:S(2)}) async-start(), calls=%async_computation.19 | async-start | bytes 3145728 | tf_op jit(solution)/shard_map/reduce_scatter | solution.py:352
  275.9 101.3 %copy-start.75 = (f32[1024]{0:T(1024)S(1)}, f32[1024]{0:T(1024)}, u32[]{:S(2)}) copy-start(f32[1024]{0:T(1024)} %convert_element_type.223) | copy-start | bytes 12292
  377.2 6.1 copy-start.4
  377.2 6.1 copy-start.26
  377.2 6.1 copy-start.28
  383.3 8.9 copy-start.55
  383.3 8.8 copy-start.71
  383.4 8.8 copy-start.76
  383.4 15.4 copy-start.43
  386.4 12.3 copy-start.59
  398.8 4.5 copy-start.30
  403.3 47.4 %copy-start.74 = (f32[1024]{0:T(1024)S(1)}, f32[1024]{0:T(1024)}, u32[]{:S(2)}) copy-start(f32[1024]{0:T(1024)} %convert_element_type.230) | copy-start | bytes 12292
  456.6 73.5 %copy-start.53 = (f32[1024]{0:T(1024)S(1)}, f32[1024]{0:T(1024)}, u32[]{:S(2)}) copy-start(f32[1024]{0:T(1024)} %convert_element_type.231) | copy-start | bytes 12292
  456.6 73.5 %copy-start.69 = (f32[1024]{0:T(1024)S(1)}, f32[1024]{0:T(1024)}, u32[]{:S(2)}) copy-start(f32[1024]{0:T(1024)} %convert_element_type.232) | copy-start | bytes 12292
  456.6 225.4 %copy-start.46 = (f32[1024]{0:T(1024)}, f32[1024]{0:T(1024)S(1)}, u32[]{:S(2)}) copy-start(f32[1024]{0:T(1024)S(1)} %broadcast_multiply_fusion.1) | copy-start | bytes 12292
  459.2 222.8 %copy-start.62 = (f32[1024]{0:T(1024)}, f32[1024]{0:T(1024)S(1)}, u32[]{:S(2)}) copy-start(f32[1024]{0:T(1024)S(1)} %fusion.59) | copy-start | bytes 12292
  459.2 150.0 %copy-start.64 = (f32[32,1,128]{2,1,0:T(1,128)S(1)}, f32[32,1,128]{2,1,0:T(1,128)}, u32[]{:S(2)}) copy-start(f32[32,1,128]{2,1,0:T(1,128)} %convert_element_type.267) | copy-start | bytes 49156
  459.2 150.0 %copy-start.73 = (f32[1024]{0:T(1024)S(1)}, f32[1024]{0:T(1024)}, u32[]{:S(2)}) copy-start(f32[1024]{0:T(1024)} %convert_element_type.236) | copy-start | bytes 12292
  627.3 4.0 copy-start.50
  665.6 16.5 copy-start.20
  685.5 4.0 copy-start.9
  703.9 5.8 copy-start.1
  716.2 5.5 copy-start.6
  734.4 5.8 copy-start.1
  746.7 5.5 copy-start.6
  752.2 3.4 copy-start.44
  752.2 3.4 copy-start.56
  752.2 3.4 copy-start.60
  755.6 380.4 %reduce-scatter.12.cloned.1.call-start = ((), (), s32[]{:S(2)}) async-start(), calls=%async_computation.18 | async-start | bytes 12582912 | tf_op jit(solution)/shard_map/reduce_scatter | solution.py:417
  755.6 6.5 copy-start.49
  755.7 6.5 copy-start.18
  766.0 4.8 copy-start.25
  767.1 5.3 copy-start.27
  767.1 5.3 copy-start.29
  893.6 3.6 copy-start.2
  1021.9 3.6 copy-start.2
  1038.0 247.9 %all-reduce.36.cloned.1.call-start = ((), (), s32[]{:S(2)}) async-start(), calls=%async_computation.27 | async-start | bytes 155648
  1140.9 9.8 copy-start.42
  1140.9 11.8 copy-start.36
  1155.5 279.0 %reduce-scatter.22.cloned.1.call-start = ((), (), s32[]{:S(2)}) async-start(), calls=%async_computation.23 | async-start | bytes 4325376 | tf_op jit(solution)/shard_map/reduce_scatter | solution.py:377
  1162.8 412.8 %reduce-scatter.20.cloned.1.call-start = ((), (), s32[]{:S(2)}) async-start(), calls=%async_computation.22 | async-start | bytes 4325376 | tf_op jit(solution)/shard_map/reduce_scatter | solution.py:373
  1170.9 545.7 %reduce-scatter.18.cloned.1.call-start = ((), (), s32[]{:S(2)}) async-start(), calls=%async_computation.21 | async-start | bytes 4325376 | tf_op jit(solution)/shard_map/reduce_scatter | solution.py:446
  1177.6 721.9 %reduce-scatter.28.cloned.1.call-start = ((), (), s32[]{:S(2)}) async-start(), calls=%async_computation.26 | async-start | bytes 8650752
  1193.7 1066.4 %reduce-scatter.26.cloned.1.call-start = ((), (), s32[]{:S(2)}) async-start(), calls=%async_computation.25 | async-start | bytes 17301504 | tf_op jit(solution)/shard_map/reduce_scatter | solution.py:307
  1214.6 1406.7 %reduce-scatter.24.cloned.1.call-start = ((), (), s32[]{:S(2)}) async-start(), calls=%async_computation.24 | async-start | bytes 17301504 | tf_op jit(solution)/shard_map/reduce_scatter | solution.py:305
  1232.1 1552.3 %reduce-scatter.16.cloned.1.call-start = ((), (), s32[]{:S(2)}) async-start(), calls=%async_computation.20 | async-start | bytes 12976128 | tf_op jit(solution)/shard_map/reduce_scatter | solution.py:443
  1244.9 4.4 copy-start.40
  1244.9 4.4 copy-start.11
  (43 other events, 66.9 us)
Sparse Core Ops, SparseCore 0:
  10.9 72.8 all-gather.10
  85.4 19.8 all-gather.16
  108.2 62.0 all-gather.18
  171.7 102.5 all-gather.12
  277.3 56.4 all-gather.14
  336.8 55.3 all-gather.20
  395.3 55.3 all-gather.22
  453.8 76.2 all-gather.24
  533.2 76.0 all-gather.26
  755.7 30.4 reduce-scatter.13
  1038.1 97.8 reduce-scatter.11
  1155.7 130.1 all-reduce.35
  1290.0 144.4 reduce-scatter.21
  1437.3 138.2 reduce-scatter.19
  1578.3 138.3 reduce-scatter.17
  1719.4 180.1 reduce-scatter.27
  1902.3 357.7 reduce-scatter.25
  2262.8 358.4 reduce-scatter.23
  2627.9 156.4 reduce-scatter.15
where the time goes:
time: 2800 us; the launch traced here: 2790 us
  waiting for transfers between devices  1860 us (66%)
  matrix products  464 us (17%)
  local copies, waits for them, and re-layouts  182 us (6%)
  other arithmetic  158 us (6%)
  blocking collectives  109 us (4%)
    reduce_scatter x1, waiting for transfers between devices, on_device(): lax.psum_scatter(grad_up, ('dp', 'seq'), scatter_dimension=0, tiled=True)  361 us
    reduce_scatter x1, waiting for transfers between devices, on_device(): lax.psum_scatter(grad_down, ('dp', 'seq'), scatter_dimension=0, tiled=True)  361 us
    unnamed x21, waiting for transfers between devices  219 us
    reduce_scatter x1, waiting for transfers between devices, on_device(): lax.psum_scatter(grad_ainputs, ('dp', 'seq'), scatter_dimension=0, tiled=...  163 us
    reduce_scatter x1, waiting for transfers between devices, on_device(): lax.psum_scatter(grad_cquery, ('dp', 'seq'), scatter_dimension=0, tiled=T...  141 us
    reduce_scatter x1, waiting for transfers between devices, on_device(): lax.psum_scatter(grad_aoutput, ('dp', 'seq'), scatter_dimension=0, tiled=...  141 us
    reduce_scatter x1, waiting for transfers between devices, on_device(): lax.psum_scatter(grad_coutput, ('dp', 'seq'), scatter_dimension=0, tiled=...  129 us
    reduce_scatter x1, waiting for transfers between devices, on_device(): lax.psum_scatter(jnp.concatenate([grad_sk, grad_sv], axis=-1).astype(jnp....  91.1 us
  transfers between devices with their start and end apart: 19, of which 15 were waited for; matrix products, arithmetic and copies ran while one was open for 22% of the time, Pallas kernels for 0%

commit v1 on v0

--- a/solution.py
+++ b/solution.py
@@ -1,8 +1,11 @@
+import functools
 import math
 
 import jax
 import jax.numpy as jnp
 from jax import lax
+from jax.experimental import pallas as pl
+from jax.experimental.pallas import tpu as pltpu
 from jax.sharding import PartitionSpec as P
 
 HEADS = 16
@@ -449,6 +452,1187 @@
     return (layer_out, tokens_grad, text_grad, *attn_sums, *cross_sums, *ffn_sums)
 
 
+MESH_ID = pl.DeviceIdType.MESH
+ANYWHERE = pl.BlockSpec(memory_space=pl.ANY)
+VMEM_LIMIT = 56 * 2**20
+
+
+class Place:
+    def __init__(self, depth):
+        group = lax.axis_index("dp")
+        self.depth = depth
+        self.z = group // 4
+        self.x = lax.rem(group // 2, 2)
+        self.core = lax.rem(group, 2)
+        self.y = lax.axis_index("seq")
+
+    def device(self, z, x, core, y):
+        return {"dp": (z * 2 + x) * 2 + core, "seq": y}
+
+    def along_z(self, step):
+        return self.device(lax.rem(self.z + step, self.depth), self.x, self.core, self.y)
+
+    def across_x(self):
+        return self.device(self.z, 1 - self.x, self.core, self.y)
+
+    def across_y(self):
+        return self.device(self.z, self.x, self.core, 1 - self.y)
+
+    def sibling(self):
+        return self.device(self.z, self.x, 1 - self.core, self.y)
+
+    def along(self, axis):
+        if axis == "z":
+            return [self.along_z(step) for step in range(1, self.depth)]
+        return [self.across_x() if axis == "x" else self.across_y()]
+
+    def greet(self):
+        partners = [self.along_z(step) for step in range(1, self.depth)]
+        partners += [self.across_x(), self.across_y(), self.sibling()]
+        barrier = pltpu.get_barrier_semaphore()
+        for partner in partners:
+            pl.semaphore_signal(barrier, inc=1, device_id=partner, device_id_type=MESH_ID)
+        pl.semaphore_wait(barrier, len(partners))
+
+
+def remote(source, target, sems, item, index, device):
+    send, receive = sems
+    return pltpu.make_async_remote_copy(
+        src_ref=source,
+        dst_ref=target,
+        send_sem=send.at[item, index],
+        recv_sem=receive.at[item, index],
+        device_id=device,
+        device_id_type=MESH_ID,
+    )
+
+
+def pipelined(phase_lists):
+    count = max(len(phases) + first for first, phases in enumerate(phase_lists))
+    stages = []
+    for turn in range(count):
+        work = [
+            phases[turn - first]
+            for first, phases in enumerate(phase_lists)
+            if 0 <= turn - first < len(phases)
+        ]
+        stages.append(work)
+    return stages
+
+
+ORDERS = (("z", "x", "y"), ("z", "y", "x"))
+
+
+def gather_phases(place, shard, whole, rows, cols, sems, local, stop, item):
+    half = rows.size // 2
+    halves = (pl.ds(rows.start, half), pl.ds(rows.start + half, half))
+    here = {"z": place.z, "x": place.x, "y": place.y}
+    every = slice(None)
+
+    def view(done, some_rows, core):
+        at = {axis: every if axis in done else here[axis] for axis in here}
+        return whole.at[at["z"], at["x"], core, at["y"], some_rows, cols]
+
+    def copies(phase):
+        made = []
+        if phase == 3:
+            both = view("zxy", rows, place.core)
+            return [remote(both, both, sems, item, 2 * place.depth + 2, place.sibling())]
+        slot = sum(len(place.along(o[p])) for o in ORDERS for p in range(phase))
+        for some_rows, order in zip(halves, ORDERS):
+            target = view(order[:phase], some_rows, place.core)
+            source = shard.at[some_rows, cols] if phase == 0 else target
+            for device in place.along(order[phase]):
+                made.append(remote(source, target, sems, item, slot, device))
+                slot += 1
+        return made
+
+    def take():
+        return pltpu.make_async_copy(shard.at[rows, cols], stop, local.at[item, 0])
+
+    def put():
+        return pltpu.make_async_copy(stop, view("", rows, place.core), local.at[item, 1])
+
+    def start(phase):
+        for copy in copies(phase):
+            copy.start()
+
+    def wait(phase):
+        for copy in copies(phase):
+            copy.wait()
+
+    def opening():
+        start(0)
+        take().start()
+        take().wait()
+        put().start()
+
+    def turn(phase):
+        def run():
+            wait(phase - 1)
+            if phase == 1:
+                put().wait()
+            start(phase)
+
+        return run
+
+    return [opening, turn(1), turn(2), turn(3), lambda: wait(3)]
+
+
+def swap_phases(place, source, target, sems, local, stop, item):
+    y = place.y
+
+    def away():
+        return remote(source.at[1 - y], target.at[y], sems, item, 0, place.across_y())
+
+    def take():
+        return pltpu.make_async_copy(source.at[y], stop, local.at[item, 0])
+
+    def put():
+        return pltpu.make_async_copy(stop, target.at[y], local.at[item, 1])
+
+    def opening():
+        away().start()
+        take().start()
+
+    def middle():
+        take().wait()
+        put().start()
+
+    def closing():
+        put().wait()
+        away().wait()
+
+    return [opening, middle, closing]
+
+
+def sum_scratch(depth, slots, items, rows, cols, dtype):
+    half = rows // 2
+    return [
+        pltpu.VMEM((slots, depth, 2, 2, rows, cols), dtype),
+        pltpu.VMEM((items, depth, 2, 2, rows, cols), dtype),
+        pltpu.VMEM((items, depth, 2, half, cols), dtype),
+        pltpu.VMEM((items, depth, half, cols), dtype),
+        pltpu.VMEM((items, depth - 1, half, cols), dtype),
+        pltpu.VMEM((items, depth, 2, half, cols), dtype),
+        pltpu.VMEM((items, depth - 1, 2, half, cols), dtype),
+        pltpu.VMEM((items, half, cols), dtype),
+    ]
+
+
+def sum_phases(place, source, result, rows, cols, bufs, sems, local, item, slots):
+    own = bufs[0].at[item % slots]
+    came, a_y, a_x, a_z, b_x, b_z, b_y = (buf.at[item] for buf in bufs[1:])
+    depth = place.depth
+    half = rows.size // 2
+    low, high = pl.ds(0, half), pl.ds(half, half)
+    z, x, core, y = place.z, place.x, place.core, place.y
+    every = slice(None)
+
+    def load():
+        return pltpu.make_async_copy(
+            source.at[every, every, core, every, rows, cols], own, local.at[item, 0]
+        )
+
+    def send(a, b, index, device):
+        return remote(a, b, sems, item, index, device)
+
+    def copies(phase):
+        if phase == 0:
+            theirs = source.at[every, every, 1 - core, every, rows, cols]
+            return [send(theirs, came, 0, place.sibling())]
+        if phase == 1:
+            return [
+                send(own.at[every, every, 1 - y, low], a_y, 1, place.across_y()),
+                send(own.at[every, 1 - x, every, high], b_x, 2, place.across_x()),
+            ]
+        if phase == 2:
+            return [send(a_y.at[every, 1 - x], a_x, 3, place.across_x())] + [
+                send(
+                    b_x.at[lax.rem(z + step, depth)], b_z.at[step - 1], 3 + step,
+                    place.along_z(step),
+                )
+                for step in range(1, depth)
+            ]
+        return [send(b_z.at[0, 1 - y], b_y, 3 + depth, place.across_y())] + [
+            send(
+                a_x.at[lax.rem(z + step, depth)], a_z.at[step - 1], 3 + depth + step,
+                place.along_z(step),
+            )
+            for step in range(1, depth)
+        ]
+
+    def start(phase):
+        for copy in copies(phase):
+            copy.start()
+
+    def wait(phase):
+        for copy in copies(phase):
+            copy.wait()
+
+    def opening():
+        load().start()
+        start(0)
+
+    def after_core():
+        load().wait()
+        wait(0)
+
+        @pl.loop(0, depth)
+        def _(k):
+            for i in range(2):
+                for j in range(2):
+                    own[k, i, j] = own[k, i, j] + came[k, i, j]
+
+        start(1)
+
+    def after_one():
+        wait(1)
+
+        @pl.loop(0, depth)
+        def _(k):
+            for i in range(2):
+                a_y[k, i] = a_y[k, i] + own[k, i, y, low]
+                b_x[k, i] = b_x[k, i] + own[k, x, i, high]
+
+        start(2)
+
+    def wide(values):
+        return values.astype(jnp.float32)
+
+    def after_two():
+        wait(2)
+
+        @pl.loop(0, depth)
+        def _(k):
+            a_x[k] = a_x[k] + a_y[k, x]
+
+        for i in range(2):
+            total = wide(b_x[z, i])
+            for step in range(1, depth):
+                total = total + wide(b_z[step - 1, i])
+            b_z[0, i] = total.astype(b_z.dtype)
+        start(3)
+
+    def closing():
+        wait(3)
+        total = wide(a_x[z])
+        for step in range(1, depth):
+            total = total + wide(a_z[step - 1])
+        result[pl.ds(rows.start, half), cols] = total
+        result[pl.ds(rows.start + half, half), cols] = wide(b_z[0, y]) + wide(b_y[...])
+
+    return [opening, after_core, after_one, after_two, closing]
+
+
+def copy_sems(items, depth):
+    width = 2 * depth + 3
+    return [
+        pltpu.SemaphoreType.DMA((items, width)),
+        pltpu.SemaphoreType.DMA((items, width)),
+        pltpu.SemaphoreType.DMA((items, 2)),
+    ]
+
+
+ITEM = 1024
+
+
+def weight_items(shape):
+    rows, cols = shape
+    return [
+        (pl.ds(r, 32), pl.ds(c, min(ITEM, cols)))
+        for r in range(0, rows, 32)
+        for c in range(0, cols, min(ITEM, cols))
+    ]
+
+
+def merged(stage_lists):
+    count = max(len(stages) for stages in stage_lists)
+    return [
+        [one for stages in stage_lists if turn < len(stages) for one in stages[turn]]
+        for turn in range(count)
+    ]
+
+
+class Swap:
+    def __init__(self, depth, arrays):
+        self.depth = depth
+        self.arrays = list(arrays)
+        self.in_specs = [ANYWHERE] * len(arrays)
+        self.out_shape = [jax.ShapeDtypeStruct(a.shape, a.dtype) for a in arrays]
+        self.out_specs = [ANYWHERE] * len(arrays)
+        self.scratch = copy_sems(len(arrays), depth)
+        self.scratch += [pltpu.VMEM(a.shape[1:], a.dtype) for a in arrays]
+
+    def stages(self, place, ins, outs, scratch):
+        phases = [
+            swap_phases(place, a, b, scratch[:2], scratch[2], scratch[3 + k], k)
+            for k, (a, b) in enumerate(zip(ins, outs))
+        ]
+        opening, middle, closing = (list(part) for part in zip(*phases))
+        return [opening, middle, [], [], closing]
+
+    def finish(self, results):
+        return list(results)
+
+
+class Gather:
+    def __init__(self, depth, shards):
+        self.depth = depth
+        self.arrays = list(shards)
+        self.order = [
+            (index, rows, cols)
+            for index, shard in enumerate(shards)
+            for rows, cols in weight_items(shard.shape)
+        ]
+        self.in_specs = [ANYWHERE] * len(shards)
+        self.out_shape = [
+            jax.ShapeDtypeStruct((depth, 2, 2, 2) + s.shape, s.dtype) for s in shards
+        ]
+        self.out_specs = [ANYWHERE] * len(shards)
+        self.scratch = copy_sems(len(self.order), depth)
+        self.scratch += [
+            pltpu.VMEM((rows.size, cols.size), shards[index].dtype)
+            for index, rows, cols in self.order
+        ]
+
+    def stages(self, place, ins, outs, scratch):
+        return pipelined(
+            [
+                gather_phases(
+                    place, ins[index], outs[index], rows, cols, scratch[:2], scratch[2],
+                    scratch[3 + item], item,
+                )
+                for item, (index, rows, cols) in enumerate(self.order)
+            ]
+        )
+
+    def finish(self, results):
+        return [r.reshape(-1, r.shape[-1]) for r in results]
+
+
+SLOTS = 4
+
+
+class Total:
+    def __init__(self, depth, grads):
+        self.depth = depth
+        shards = depth * 8
+        shapes = [(g.shape[0] // shards, g.shape[1]) for g in grads]
+        self.arrays = [g.reshape((depth, 2, 2, 2) + s) for g, s in zip(grads, shapes)]
+        self.order = [
+            (index, rows, cols)
+            for index, shape in enumerate(shapes)
+            for rows, cols in weight_items(shape)
+        ]
+        self.in_specs = [ANYWHERE] * len(grads)
+        self.out_shape = [jax.ShapeDtypeStruct(s, jnp.float32) for s in shapes]
+        self.out_specs = [whole_block(s) for s in shapes]
+        rows, cols = self.order[0][1].size, self.order[0][2].size
+        self.slots = min(SLOTS, len(self.order))
+        self.scratch = copy_sems(len(self.order), depth) + sum_scratch(
+            depth, self.slots, len(self.order), rows, cols, grads[0].dtype
+        )
+
+    def stages(self, place, ins, outs, scratch):
+        return pipelined(
+            [
+                sum_phases(
+                    place, ins[index], outs[index], rows, cols, scratch[3:], scratch[:2],
+                    scratch[2], item, self.slots,
+                )
+                for item, (index, rows, cols) in enumerate(self.order)
+            ]
+        )
+
+    def finish(self, results):
+        return list(results)
+
+
+def whole_block(shape):
+    return pl.BlockSpec(shape, lambda *_: (0,) * len(shape))
+
+
+def hosted(name, number, comms, steps, body, args, in_specs, out_shape, out_specs, scratch):
+    depth = comms[0].depth
+    all_args = list(args)
+    all_in, all_shape, all_out, all_scratch = (
+        list(in_specs), list(out_shape), list(out_specs), list(scratch),
+    )
+    for comm in comms:
+        all_args += comm.arrays
+        all_in += comm.in_specs
+        all_shape += comm.out_shape
+        all_out += comm.out_specs
+        all_scratch += comm.scratch
+
+    def kernel(*refs):
+        refs = list(refs)
+
+        def take(count):
+            taken = refs[:count]
+            del refs[:count]
+            return taken
+
+        own_in = take(len(args))
+        comm_in = [take(len(comm.arrays)) for comm in comms]
+        own_out = take(len(out_shape))
+        comm_out = [take(len(comm.out_shape)) for comm in comms]
+        own_scratch = take(len(scratch))
+        comm_scratch = [take(len(comm.scratch)) for comm in comms]
+        place = Place(depth)
+        stages = merged(
+            [
+                comm.stages(place, a, b, c)
+                for comm, a, b, c in zip(comms, comm_in, comm_out, comm_scratch)
+            ]
+        )
+        step = pl.program_id(0)
+
+        @pl.when(step == 0)
+        def _():
+            place.greet()
+
+        spread = max(1, len(stages) - 1)
+        for at in range(steps):
+            due = [k for k in range(len(stages) - 1) if k * steps // spread == at]
+            if due:
+
+                @pl.when(step == at)
+                def _(due=due):
+                    for k in due:
+                        for one in reversed(stages[k]):
+                            one()
+
+        if body is not None:
+            body(*own_in, *own_out, *own_scratch)
+
+        @pl.when(step == steps - 1)
+        def _():
+            for one in reversed(stages[-1]):
+                one()
+
+    results = pl.pallas_call(
+        kernel,
+        grid=(steps,),
+        out_shape=all_shape,
+        in_specs=all_in,
+        out_specs=all_out,
+        scratch_shapes=all_scratch,
+        compiler_params=pltpu.CompilerParams(
+            collective_id=number, has_side_effects=True, vmem_limit_bytes=VMEM_LIMIT
+        ),
+        name=name,
+    )(*all_args)
+    results = list(results)
+    own = results[: len(out_shape)]
+    results = results[len(out_shape) :]
+    finished = []
+    for comm in comms:
+        finished.append(comm.finish(results[: len(comm.out_shape)]))
+        results = results[len(comm.out_shape) :]
+    return own, finished
+
+
+def only(name, number, comms):
+    return hosted(name, number, comms, 1, None, [], [], [], [], [])[1]
+
+
+QB=256
+def nt(a,b): return lax.dot_general(a,b,(((1,),(1,)),((),())),preferred_element_type=jnp.float32)
+def nn(a,b): return jnp.dot(a,b,preferred_element_type=jnp.float32)
+def half_mask(rows):
+    lane=lax.broadcasted_iota(jnp.int32,(rows,128),1)
+    return lane<64
+def pick(block,h,first):
+    zero=jnp.zeros_like(block)
+    return jnp.where(first,block,zero) if h==0 else jnp.where(first,zero,block)
+def scores(keys, queries, diagonal, bias):
+    s = nt(keys, queries)
+    if diagonal:
+        r = lax.broadcasted_iota(jnp.int32, s.shape, 0)
+        c = lax.broadcasted_iota(jnp.int32, s.shape, 1)
+        s = jnp.where(r <= c, s, MASKED)
+    if bias is not None:
+        s = s + bias
+    return s
+
+
+def segments(causal,qb,keys):
+    if not causal: return [(0,keys,False)]
+    out=[]
+    if qb>0: out.append((0,qb*QB,False))
+    out.append((qb*QB,(qb+1)*QB,True))
+    return out
+def attend_pair(causal, rows, keys, get_q, get_k, get_v, bias, put, lse_ref):
+    vt = get_v(0, keys).T
+    first = half_mask(QB)
+    for qb in range(rows // QB):
+        sl = slice(qb * QB, (qb + 1) * QB)
+        q = get_q(qb * QB, (qb + 1) * QB) * jnp.bfloat16(0.125)
+        outs = []
+        for h in (0, 1):
+            qs = pick(q, h, first)
+            segs = segments(causal, qb, keys)
+            ss = [scores(get_k(lo, hi), qs, d, bias) for lo, hi, d in segs]
+            m = functools.reduce(jnp.maximum, [jnp.max(s, axis=0, keepdims=True) for s in ss])
+            ps = [jnp.exp(s - m) for s in ss]
+            l = functools.reduce(jnp.add, [jnp.sum(p, axis=0, keepdims=True) for p in ps])
+            ot = functools.reduce(
+                jnp.add,
+                [
+                    nn(vt[h * 64 : (h + 1) * 64, lo:hi], p.astype(jnp.bfloat16))
+                    for p, (lo, hi, _) in zip(ps, segs)
+                ],
+            )
+            outs.append(ot * (1.0 / l))
+            lse_ref[h : h + 1, sl] = m + jnp.log(l)
+        put(sl, jnp.concatenate(outs, axis=0).T.astype(jnp.bfloat16))
+
+
+def bwd_body(causal,q_ref,k_ref,v_ref,bias,o_ref,do_ref,lse_ref,dq_ref,dk_ref,dv_ref,dk_acc,dv_acc):
+    rows=q_ref.shape[0]; keys=k_ref.shape[0]
+    kt=(k_ref[...]*jnp.bfloat16(0.125)).T
+    first=half_mask(QB)
+    nq=rows//QB
+    order=list(range(nq))[::-1] if causal else list(range(nq))
+    started=set()
+    for qb in order:
+        sl=slice(qb*QB,(qb+1)*QB)
+        q=q_ref[sl,:]*jnp.bfloat16(0.125)
+        do=do_ref[sl,:]
+        dt=(do.astype(jnp.float32)*o_ref[sl,:].astype(jnp.float32)).T
+        outs=[]
+        segs=segments(causal,qb,keys)
+        new={}
+        for h in (0,1):
+            qs=pick(q,h,first); doh=pick(do,h,first)
+            delta=jnp.sum(dt[h*64:(h+1)*64,:],axis=0,keepdims=True)
+            lse=lse_ref[0,h:h+1,sl]
+            dqt=None
+            for lo,hi,d in segs:
+                p=jnp.exp(scores(k_ref[lo:hi,:],qs,d,bias)-lse)
+                dp=nt(v_ref[lo:hi,:],doh)
+                ds=(p*(dp-delta)).astype(jnp.bfloat16)
+                t=nn(kt[h*64:(h+1)*64,lo:hi],ds)
+                dqt=t if dqt is None else dqt+t
+                a=nn(p.astype(jnp.bfloat16),doh); b=nn(ds,qs)
+                if (lo,hi) in new: new[(lo,hi)]=(new[(lo,hi)][0]+a,new[(lo,hi)][1]+b)
+                else: new[(lo,hi)]=(a,b)
+            outs.append(dqt)
+        dq_ref[sl,:]=jnp.concatenate(outs,axis=0).T.astype(jnp.bfloat16)
+        for (lo,hi),(a,b) in new.items():
+            if qb==order[0]:
+                dv_acc[lo:hi,:]=a; dk_acc[lo:hi,:]=b
+            else:
+                dv_acc[lo:hi,:]+=a; dk_acc[lo:hi,:]+=b
+    dk_ref[...]=dk_acc[...].astype(jnp.bfloat16)
+    dv_ref[...]=dv_acc[...].astype(jnp.bfloat16)
+def self_attend_back(qkv,o,do,lse,number,comms):
+    R=qkv.shape[0]; D=qkv.shape[1]//3; n=D//128
+    def body(q,k,v,o,do,lse,dq,dk,dv,ka,va): bwd_body(True,q,k,v,None,o,do,lse,dq,dk,dv,ka,va)
+    blk=pl.BlockSpec((R,128),lambda j:(0,j))
+    return hosted("self_attend_back",number,comms,n,body,[qkv]*3+[o,do,lse],
+        [pl.BlockSpec((R,128),lambda j,i=i:(0,j+n*i)) for i in range(3)]+[blk,blk,pl.BlockSpec((1,2,R),lambda j:(j,0,0))],
+        [jax.ShapeDtypeStruct((R,D),jnp.bfloat16)]*3,[blk]*3,[pltpu.VMEM((R,128),jnp.float32)]*2)
+def cross_attend_back(q,kv,bias,o,do,lse,number,comms):
+    R,D=q.shape; T=kv.shape[0]; n=D//128
+    def body(q,k,v,b,o,do,lse,dq,dk,dv,ka,va): bwd_body(False,q,k,v,jnp.concatenate([b[...]]*2,axis=1),o,do,lse,dq,dk,dv,ka,va)
+    blk=pl.BlockSpec((R,128),lambda j:(0,j)); tb=pl.BlockSpec((T,128),lambda j:(0,j))
+    return hosted("cross_attend_back",number,comms,n,body,[q,kv,kv,bias,o,do,lse],
+        [blk]+[pl.BlockSpec((T,128),lambda j,i=i:(0,j+n*i)) for i in range(2)]+[pl.BlockSpec((T,128),lambda j:(0,0)),blk,blk,pl.BlockSpec((1,2,R),lambda j:(j,0,0))],
+        [jax.ShapeDtypeStruct((R,D),jnp.bfloat16)]+[jax.ShapeDtypeStruct((T,D),jnp.bfloat16)]*2,[blk,tb,tb],[pltpu.VMEM((T,128),jnp.float32)]*2)
+
+
+BLOCK = 256
+MATMUL_ROWS = 512
+RING = 6
+
+VECTOR_COUNT = 15
+(
+    A_GAIN, A_SHIFT, A_QBIAS, A_VBIAS, A_OBIAS, C_GAIN, C_SHIFT, C_QBIAS, C_VBIAS, C_OBIAS,
+    F_GAIN, F_SHIFT, F_DOWNBIAS, Z_GAIN, Z_SHIFT,
+) = range(VECTOR_COUNT)
+F_UPBIAS = VECTOR_COUNT
+
+
+def block_rows(index, size):
+    return pl.ds(pl.multiple_of(index * size, size), size)
+
+
+def lanes(index, size):
+    return pl.ds(pl.multiple_of(index * size, size), size)
+
+
+def center_and_scale(values):
+    center = values - jnp.mean(values, axis=-1, keepdims=True)
+    spread = jnp.mean(center * center, axis=-1, keepdims=True)
+    scale = lax.rsqrt(spread + EPSILON)
+    return center * scale, scale
+
+
+def norm_pull(unit, scale, pulled):
+    inner = jnp.mean(pulled * unit, axis=-1, keepdims=True)
+    return scale * (pulled - jnp.mean(pulled, axis=-1, keepdims=True) - unit * inner)
+
+
+def gelu_and_slope(values):
+    root = math.sqrt(2.0 / math.pi)
+    square = values * values
+    bend = jnp.tanh(root * (values + 0.044715 * (values * square)))
+    rise = root * (1.0 + 3.0 * 0.044715 * square)
+    result = 0.5 * values * (1.0 + bend)
+    slope = 0.5 * (1.0 + bend) + 0.5 * values * ((1.0 - bend * bend) * rise)
+    return result, slope
+
+
+def spread_vectors(packed):
+    rows = packed.shape[0]
+    width = rows
+    lane = lax.broadcasted_iota(jnp.int32, (128, width), 1)
+    source = lax.broadcasted_iota(jnp.int32, (128, width), 0)
+    select = jnp.where(lax.rem(lane, 32) == source, 1.0, 0.0).astype(jnp.bfloat16)
+    wide = jnp.dot(packed, select, preferred_element_type=jnp.float32)
+    row = lax.broadcasted_iota(jnp.int32, (rows, width), 0)
+    lane = lax.broadcasted_iota(jnp.int32, (rows, width), 1)
+    wide = jnp.where(row // 32 == lane // 32, wide, 0.0)
+    return jnp.sum(wide.reshape(rows // 32, 32, width), axis=0)
+
+
+class Copies:
+    def __init__(self, sems):
+        self.sems = sems
+        self.open = {}
+        self.used = 0
+
+    def start(self, source, target):
+        copy = pltpu.make_async_copy(source, target, self.sems.at[self.used])
+        self.used += 1
+        copy.start()
+        return copy
+
+
+def forward_kernel(depth, sizes, *refs):
+    refs = list(refs)
+
+    def take(count):
+        taken = refs[:count]
+        del refs[:count]
+        return taken
+
+    shard_count = len(sizes)
+    tokens, texts, cots, unit_length, text_length = take(5)
+    shards = take(shard_count)
+    wholes = take(shard_count)
+    (
+        o_tokens, o_text, o_h1, o_qkv, o_o1, o_after_self, o_h2, o_cq, o_ckv, o_o2,
+        o_after_cross, o_h3, o_active, o_slope, o_gaf, o_gbr, o_layer,
+    ) = take(17)
+    vec, lse1, lse2, zgrads = take(4)
+    tok, txt, cot, x, o1, cq, ckv, o2, resid, h2, ring, slopes, packed = take(13)
+    stops = take(sum(len(weight_items(s)) for s in sizes))
+    send, receive, local, sw_send, sw_receive, sw_local, loads, outs = take(8)
+
+    place = Place(depth)
+    y = place.y
+    rows = resid.shape[0]
+    width = resid.shape[1]
+    part = rows // 2
+    copies = Copies(outs)
+    phases, chunks, item = [], [], 0
+    for index, size in enumerate(sizes):
+        for r, c in weight_items(size):
+            phase = gather_phases(
+                place, shards[index], wholes[index], r, c, (send, receive), local, stops[item], item
+            )
+            phases.append(phase)
+            if index > 0:
+                chunks.append((wholes[index], c))
+            item += 1
+    first = phases[0]
+    stages = pipelined(phases[1:])
+    stages = [([first[k]] if k < len(first) else []) + s for k, s in enumerate(stages)]
+
+    def swapping(k, source, target):
+        def away():
+            return remote(source.at[1 - y], target.at[y], (sw_send, sw_receive), k, 0, place.across_y())
+
+        def home():
+            return pltpu.make_async_copy(source.at[y], target.at[y], sw_local.at[k])
+
+        def opening():
+            away().start()
+            home().start()
+
+        def closing():
+            away().wait()
+            home().wait()
+
+        return opening, closing
+
+    token_swap = swapping(0, tokens, tok)
+    text_swap = swapping(1, texts, txt)
+    cot_swap = swapping(2, cots, cot)
+
+    def load(chunk):
+        whole, cols = chunks[chunk]
+        return pltpu.make_async_copy(
+            whole.at[:, :, :, :, :, cols], ring.at[chunk % RING], loads.at[chunk]
+        )
+
+    def stage(k):
+        for one in reversed(stages[k]):
+            one()
+        if k >= 4:
+            load(k - 4).start()
+
+    def weight(chunk):
+        return ring[chunk % RING].reshape(width, width)
+
+    def row(index):
+        return vec[index : index + 1, :]
+
+    def looped(count, body, due=()):
+        @pl.loop(0, count)
+        def _(j):
+            for at, k in due:
+
+                @pl.when(j == at)
+                def _(k=k):
+                    stage(k)
+
+            body(j)
+
+    place.greet()
+    token_swap[0]()
+    for k in range(3):
+        stage(k)
+    text_swap[0]()
+    stage(3)
+    stage(4)
+    pack = pltpu.make_async_copy(wholes[0], packed, outs.at[copies.used])
+    copies.used += 1
+    pack.start()
+    pack.wait()
+    vec[...] = spread_vectors(packed[...].reshape(-1, 128))
+    token_swap[1]()
+    done_tokens = copies.start(tok, o_tokens)
+
+    def token_block(b):
+        half = b // (part // BLOCK)
+        inner = lax.rem(b, part // BLOCK)
+        return tok[half, block_rows(inner, BLOCK), :].astype(jnp.float32)
+
+    def norm_one(b):
+        unit, _ = center_and_scale(token_block(b))
+        at = block_rows(b, BLOCK)
+        x[at, 3 * width :] = (unit * row(A_GAIN) + row(A_SHIFT)).astype(jnp.bfloat16)
+        resid[at, :] = token_block(b)
+
+    looped(rows // BLOCK, norm_one)
+    done_h1 = copies.start(x.at[:, pl.ds(3 * width, width)], o_h1)
+
+    def project(chunk):
+        bias = (row(A_QBIAS), None, row(A_VBIAS))[chunk]
+        load(chunk).wait()
+
+        def block(b):
+            at = block_rows(b, MATMUL_ROWS)
+            value = nn(x[at, 3 * width :], weight(chunk))
+            if bias is not None:
+                value = value + bias
+            x[at, chunk * width : (chunk + 1) * width] = value.astype(jnp.bfloat16)
+
+        looped(rows // MATMUL_ROWS, block)
+
+    project(0)
+    stage(5)
+    project(1)
+    stage(6)
+    project(2)
+    done_qkv = copies.start(x.at[:, pl.ds(0, 3 * width)], o_qkv)
+    pairs = width // 128
+
+    def self_pair(j):
+        def part_of(base):
+            return lambda lo, hi: x[lo:hi, lanes(j + base * pairs, 128)]
+
+        def put(sl, value):
+            o1[sl, lanes(j, 128)] = value
+
+        attend_pair(
+            True, rows, rows, part_of(0), part_of(1), part_of(2), None, put, lse1.at[j]
+        )
+
+    looped(pairs, self_pair, ((2, 7), (4, 8), (7, 9)))
+    done_o1 = copies.start(o1, o_o1)
+    load(3).wait()
+
+    def out_block(b):
+        at = block_rows(b, MATMUL_ROWS)
+        resid[at, :] = resid[at, :] + nn(o1[at, :], weight(3)) + row(A_OBIAS)
+
+    looped(rows // MATMUL_ROWS, out_block)
+    done_after_self = copies.start(resid, o_after_self)
+
+    def norm_two(b):
+        at = block_rows(b, BLOCK)
+        unit, _ = center_and_scale(resid[at, :])
+        h2[at, :] = (unit * row(C_GAIN) + row(C_SHIFT)).astype(jnp.bfloat16)
+
+    looped(rows // BLOCK, norm_two)
+    done_h2 = copies.start(h2, o_h2)
+    stage(10)
+    load(4).wait()
+
+    def cq_block(b):
+        at = block_rows(b, MATMUL_ROWS)
+        cq[at, :] = (nn(h2[at, :], weight(4)) + row(C_QBIAS)).astype(jnp.bfloat16)
+
+    looped(rows // MATMUL_ROWS, cq_block)
+    done_cq = copies.start(cq, o_cq)
+    text_swap[1]()
+    cot_swap[0]()
+    done_text = copies.start(txt, o_text)
+    text = txt[...].reshape(-1, width)
+    text_rows = text.shape[0]
+    load(5).wait()
+    ckv[:, :width] = nn(text, weight(5)).astype(jnp.bfloat16)
+    load(6).wait()
+    ckv[:, width:] = (nn(text, weight(6)) + row(C_VBIAS)).astype(jnp.bfloat16)
+    done_ckv = copies.start(ckv, o_ckv)
+    bias = text_mask(text_rows, text_length[y])
+
+    def cross_pair(j):
+        def put(sl, value):
+            o2[sl, lanes(j, 128)] = value
+
+        attend_pair(
+            False, rows, text_rows,
+            lambda lo, hi: cq[lo:hi, lanes(j, 128)],
+            lambda lo, hi: ckv[lo:hi, lanes(j, 128)],
+            lambda lo, hi: ckv[lo:hi, lanes(j + pairs, 128)],
+            bias, put, lse2.at[j],
+        )
+
+    looped(pairs, cross_pair, ((1, 11), (4, 12), (7, 13)))
+    done_o2 = copies.start(o2, o_o2)
+    load(7).wait()
+    done_after_self.wait()
+
+    def cross_out_block(b):
+        at = block_rows(b, MATMUL_ROWS)
+        resid[at, :] = resid[at, :] + nn(o2[at, :], weight(7)) + row(C_OBIAS)
+
+    looped(rows // MATMUL_ROWS, cross_out_block)
+    done_after_cross = copies.start(resid, o_after_cross)
+    done_o1.wait()
+    h3 = o1
+
+    def norm_three(b):
+        at = block_rows(b, BLOCK)
+        unit, _ = center_and_scale(resid[at, :])
+        h3[at, :] = (unit * row(F_GAIN) + row(F_SHIFT)).astype(jnp.bfloat16)
+
+    looped(rows // BLOCK, norm_three)
+    done_h3 = copies.start(h3, o_h3)
+    done_h1.wait()
+    done_qkv.wait()
+    waiting = []
+
+    def up(q):
+        load(8 + q).wait()
+        slope_at = slopes.at[q % 2]
+
+        def block(b):
+            at = block_rows(b, BLOCK)
+            inner = nn(h3[at, :], weight(8 + q)) + row(F_UPBIAS + q)
+            active, slope = gelu_and_slope(inner)
+            x[at, q * width : (q + 1) * width] = active.astype(jnp.bfloat16)
+            slope_at[at, :] = slope.astype(jnp.bfloat16)
+
+        if q >= 2:
+            waiting[q - 2].wait()
+        looped(rows // BLOCK, block)
+        span = pl.ds(q * width, width)
+        waiting.append(copies.start(slope_at, o_slope.at[:, span]))
+
+    stage(14)
+    up(0)
+    up(1)
+    stage(15)
+    up(2)
+    up(3)
+    done_active = copies.start(x, o_active)
+    done_after_cross.wait()
+
+    def down(q):
+        load(12 + q).wait()
+
+        def block(b):
+            at = block_rows(b, MATMUL_ROWS)
+            resid[at, :] += nn(x[at, q * width : (q + 1) * width], weight(12 + q))
+
+        looped(rows // MATMUL_ROWS, block)
+
+    for q in range(4):
+        stage(16 + q)
+        down(q)
+    cot_swap[1]()
+    done_cq.wait()
+    done_o2.wait()
+    valid_count = unit_length[y]
+    zgrads[...] = jnp.zeros_like(zgrads)
+    gbr, layer = cq, o2
+
+    def last_block(b):
+        at = block_rows(b, BLOCK)
+        unit, scale = center_and_scale(resid[at, :] + row(F_DOWNBIAS))
+        position = b * BLOCK + lax.broadcasted_iota(jnp.int32, (BLOCK, 1), 0)
+        valid = jnp.where(position < valid_count, 1.0, 0.0)
+        layer[at, :] = ((unit * row(Z_GAIN) + row(Z_SHIFT)) * valid).astype(jnp.bfloat16)
+        half = b // (part // BLOCK)
+        inner = lax.rem(b, part // BLOCK)
+        upstream = cot[half, block_rows(inner, BLOCK), :].astype(jnp.float32) * valid
+        zgrads[0:1, :] += jnp.sum(upstream * unit, axis=0, keepdims=True)
+        zgrads[1:2, :] += jnp.sum(upstream, axis=0, keepdims=True)
+        grad = norm_pull(unit, scale, upstream * row(Z_GAIN))
+        low = grad.astype(jnp.bfloat16)
+        gbr[at, :] = low
+        zgrads[2:3, :] += jnp.sum(low.astype(jnp.float32), axis=0, keepdims=True)
+        resid[at, :] = grad
+
+    looped(rows // BLOCK, last_block)
+    ending = [
+        copies.start(resid, o_gaf), copies.start(gbr, o_gbr), copies.start(layer, o_layer),
+    ]
+    ending += [done_tokens, done_h2, done_text, done_ckv, done_h3, done_active]
+    for copy in ending + waiting[2:]:
+        copy.wait()
+
+
+def text_mask(text_rows, count):
+    position = lax.broadcasted_iota(jnp.int32, (text_rows, QB), 0)
+    return jnp.where(position < count, 0.0, MASKED)
+
+
+def forward(depth, number, tokens, texts, cots, unit_length, text_length, shards):
+    rows, width = 2 * tokens.shape[1], tokens.shape[2]
+    text_rows = 2 * texts.shape[1]
+    hidden = 4 * width
+    pairs = width // 128
+    sizes = [s.shape for s in shards]
+    items = sum(len(weight_items(s)) for s in sizes)
+    low, full = jnp.bfloat16, jnp.float32
+
+    def shape(*dims, kind=low):
+        return jax.ShapeDtypeStruct(dims, kind)
+
+    def vmem(*dims, kind=low):
+        return pltpu.VMEM(dims, kind)
+
+    big = shape(rows, width)
+    exact = shape(rows, width, kind=full)
+    outs = [shape(depth, 2, 2, 2, *s) for s in sizes]
+    outs += [
+        shape(*tokens.shape), shape(*texts.shape), big, shape(rows, 3 * width), big, exact, big, big,
+        shape(text_rows, 2 * width), big, exact, big, shape(rows, hidden), shape(rows, hidden),
+        exact, big, big,
+    ]
+    small = [
+        shape(32, width, kind=full), shape(pairs, 2, rows, kind=full),
+        shape(pairs, 2, rows, kind=full), shape(8, width, kind=full),
+    ]
+    scratch = [
+        vmem(*tokens.shape), vmem(*texts.shape), vmem(*cots.shape), vmem(rows, hidden),
+        vmem(rows, width), vmem(rows, width), vmem(text_rows, 2 * width), vmem(rows, width),
+        vmem(rows, width, kind=full), vmem(rows, width), vmem(RING, depth, 2, 2, 2, 32, width),
+        vmem(2, rows, width), vmem(depth, 2, 2, 2, *sizes[0]),
+    ]
+    scratch += [vmem(r.size, c.size) for s in sizes for r, c in weight_items(s)]
+    scratch += copy_sems(items, depth)
+    scratch += [
+        pltpu.SemaphoreType.DMA((3, 1)), pltpu.SemaphoreType.DMA((3, 1)),
+        pltpu.SemaphoreType.DMA((3,)), pltpu.SemaphoreType.DMA((items,)),
+        pltpu.SemaphoreType.DMA((32,)),
+    ]
+    memory = pl.BlockSpec(memory_space=pltpu.SMEM)
+    results = pl.pallas_call(
+        functools.partial(forward_kernel, depth, sizes),
+        out_shape=outs + small,
+        in_specs=[ANYWHERE] * 3 + [memory] * 2 + [ANYWHERE] * len(shards),
+        out_specs=[ANYWHERE] * len(outs) + [pl.BlockSpec(memory_space=pltpu.VMEM)] * len(small),
+        scratch_shapes=scratch,
+        compiler_params=pltpu.CompilerParams(
+            collective_id=number, has_side_effects=True, vmem_limit_bytes=VMEM_LIMIT
+        ),
+        name="forward",
+    )(tokens, texts, cots, unit_length, text_length, *shards)
+    return list(results[: len(sizes)]), list(results[len(sizes) :])
+
+
+def pack_vectors(vectors, wide):
+    packed = jnp.concatenate([jnp.stack(vectors), wide.reshape(4, -1)])
+    return jnp.pad(packed, ((0, 32 - packed.shape[0]), (0, 128 - packed.shape[1])))
+
+
+def pack_vector_grads(vectors, shards):
+    parts = jnp.concatenate([v.reshape(-1, shards, v.shape[-1] // shards) for v in vectors])
+    parts = jnp.swapaxes(parts, 0, 1)
+    parts = jnp.pad(parts, ((0, 0), (0, 32 - parts.shape[1]), (0, 128 - parts.shape[2])))
+    return parts.reshape(-1, 128)
+
+
+def half(values):
+    return values.astype(jnp.bfloat16)
+
+
+def paired_layer(
+    depth,
+    tokens,
+    text_states,
+    unit_length,
+    text_length,
+    cotangent,
+    attn_gain,
+    attn_shift,
+    attn_inputs,
+    attn_qbias,
+    attn_vbias,
+    attn_output,
+    attn_obias,
+    cross_gain,
+    cross_shift,
+    cross_query,
+    cross_qbias,
+    cross_keyval,
+    cross_vbias,
+    cross_output,
+    cross_obias,
+    ffn_gain,
+    ffn_shift,
+    ffn_up,
+    ffn_upbias,
+    ffn_down,
+    ffn_downbias,
+    final_gain,
+    final_shift,
+):
+    part_len, width = tokens.shape[1:]
+    share = attn_gain.shape[0]
+    text_part = text_states.shape[1]
+    rows = 2 * part_len
+    me = lax.axis_index("seq")
+    packed = pack_vectors(
+        [
+            attn_gain, attn_shift, attn_qbias, attn_vbias, attn_obias, cross_gain, cross_shift,
+            cross_qbias, cross_vbias, cross_obias, ffn_gain, ffn_shift, ffn_downbias, final_gain,
+            final_shift,
+        ],
+        ffn_upbias,
+    )
+    shards = depth * 8
+    up_shard = ffn_up.reshape(share, shards, 4, share).swapaxes(1, 2).reshape(share, -1)
+    wholes, kept = forward(
+        depth, 0, tokens, text_states, cotangent, unit_length, text_length,
+        [packed, attn_inputs, attn_output, cross_query, cross_keyval, cross_output, up_shard]
+        + [ffn_down[q * share : (q + 1) * share] for q in range(4)],
+    )
+    w_in, w_out, w_cq, w_ckv, w_co, w_up, *w_downs = [
+        w.reshape(-1, w.shape[-1]) for w in wholes[1:]
+    ]
+    w_down = jnp.concatenate(w_downs)
+    (
+        token_seq, text_seq, normed_one, joined, self_mixed, after_self, normed_two, cross_queries,
+        cross_kv, cross_mixed, after_cross, normed_three, active, slope, grad_after_ffn,
+        grad_branch, layer_out, vec, self_logsum, cross_logsum, zgrads,
+    ) = kept
+    inputs = to_float(token_seq).reshape(rows, width)
+    text = text_seq.reshape(2 * text_part, width)
+    allowed = jnp.arange(2 * text_part)[:, None] < text_length[me]
+    text_bias = jnp.broadcast_to(jnp.where(allowed, 0.0, MASKED), (2 * text_part, 128))
+    grad_zgain, grad_zshift, grad_downbias = zgrads[0], zgrads[1], zgrads[2]
+
+    grad_down = half(left_dot(active, grad_branch))
+    grad_active = right_dot(grad_branch, w_down)
+    grad_inner = half(grad_active * to_float(slope))
+    grad_up = half(left_dot(normed_three, grad_inner))
+    grad_upbias = jnp.sum(to_float(grad_inner), axis=0)
+    grad_normed_three = right_dot(grad_inner, w_up)
+    grad_cross_norm, grad_fgain, grad_fshift = norm_back(
+        after_cross, vec[F_GAIN], vec[F_SHIFT], grad_normed_three
+    )
+    grad_after_cross = grad_after_ffn + grad_cross_norm
+
+    cross_branch = half(grad_after_cross)
+    grad_coutput = half(left_dot(cross_mixed, cross_branch))
+    grad_cobias = jnp.sum(to_float(cross_branch), axis=0)
+    grad_cross_mixed = half(right_dot(cross_branch, w_co))
+    (grad_cq, grad_ck, grad_cv), ((s_up, *s_downs), (layer_out,)) = cross_attend_back(
+        cross_queries, cross_kv, text_bias, cross_mixed, grad_cross_mixed, cross_logsum, 3,
+        [Total(depth, [grad_up, *jnp.split(grad_down, 4)]), Swap(depth, [layer_out.reshape(2, part_len, width)])],
+    )
+    grad_ckv = jnp.concatenate([grad_ck, grad_cv], axis=-1)
+    grad_ckeyval = half(left_dot(text, grad_ckv))
+    grad_cvbias = jnp.sum(to_float(grad_cv), axis=0)
+    text_grad = half(right_dot(grad_ckv, w_ckv))
+    grad_cquery = half(left_dot(normed_two, grad_cq))
+    grad_cqbias = jnp.sum(to_float(grad_cq), axis=0)
+    grad_normed_two = right_dot(grad_cq, w_cq)
+    grad_self_norm, grad_cgain, grad_cshift = norm_back(
+        after_self, vec[C_GAIN], vec[C_SHIFT], grad_normed_two
+    )
+    grad_after_self = grad_after_cross + grad_self_norm
+
+    self_branch = half(grad_after_self)
+    grad_aoutput = half(left_dot(self_mixed, self_branch))
+    grad_aobias = jnp.sum(to_float(self_branch), axis=0)
+    grad_self_mixed = half(right_dot(self_branch, w_out))
+    (grad_q, grad_k, grad_v), ((s_ckv, s_cq, s_co), (text_grad,)) = self_attend_back(
+        joined, self_mixed, grad_self_mixed, self_logsum, 4,
+        [
+            Total(depth, [grad_ckeyval, grad_cquery, grad_coutput]),
+            Swap(depth, [text_grad.reshape(2, text_part, width)]),
+        ],
+    )
+    grad_joined = jnp.concatenate([grad_q, grad_k, grad_v], axis=-1)
+    grad_ainputs = half(left_dot(normed_one, grad_joined))
+    grad_aqbias = jnp.sum(to_float(grad_q), axis=0)
+    grad_avbias = jnp.sum(to_float(grad_v), axis=0)
+    grad_normed_one = right_dot(grad_joined, w_in)
+    grad_input_norm, grad_again, grad_ashift = norm_back(
+        inputs, vec[A_GAIN], vec[A_SHIFT], grad_normed_one
+    )
+    tokens_grad = half(grad_after_self + grad_input_norm)
+
+    small = pack_vector_grads(
+        [
+            grad_again, grad_ashift, grad_aqbias, grad_avbias, grad_aobias, grad_cgain,
+            grad_cshift, grad_cqbias, grad_cvbias, grad_cobias, grad_fgain, grad_fshift,
+            grad_downbias, grad_zgain, grad_zshift, grad_upbias.reshape(4, -1),
+        ],
+        shards,
+    )
+    (s_in, s_out), (s_small,), (tokens_grad,) = only(
+        "sum_last", 5,
+        [
+            Total(depth, [grad_ainputs, grad_aoutput]),
+            Total(depth, [small]),
+            Swap(depth, [tokens_grad.reshape(2, part_len, width)]),
+        ],
+    )
+    s_up = s_up.reshape(share, 4, shards, share).swapaxes(1, 2).reshape(share, -1)
+    s_down = jnp.concatenate(s_downs)
+    s_upbias = s_small[VECTOR_COUNT : VECTOR_COUNT + 4, :share].reshape(-1)
+    v = [s_small[i, :share] for i in range(VECTOR_COUNT)]
+    return (
+        layer_out, tokens_grad, text_grad, v[A_GAIN], v[A_SHIFT], s_in, v[A_QBIAS], v[A_VBIAS],
+        s_out, v[A_OBIAS], v[C_GAIN], v[C_SHIFT], s_cq, v[C_QBIAS], s_ckv, v[C_VBIAS], s_co,
+        v[C_OBIAS], v[F_GAIN], v[F_SHIFT], s_up, s_upbias, s_down, v[F_DOWNBIAS], v[Z_GAIN],
+        v[Z_SHIFT],
+    )
+
+
 def solution(mesh):
     in_specs = (
         P("dp", "seq", None),
@@ -508,6 +1692,15 @@
         P(("dp", "seq")),
         P(("dp", "seq")),
     )
+    groups, seq_parts = mesh.shape["dp"], mesh.shape["seq"]
+
+    def layer(*arguments):
+        shard = arguments[5].shape[0]
+        parts = arguments[0].shape[0]
+        if seq_parts == 2 and parts == 2 and groups % 4 == 0 and shard % 32 == 0:
+            return paired_layer(groups // 4, *arguments)
+        return on_device(*arguments)
+
     return jax.shard_map(
-        on_device, mesh=mesh, in_specs=in_specs, out_specs=out_specs, check_vma=False
-    )
+        layer, mesh=mesh, in_specs=in_specs, out_specs=out_specs, check_vma=False
+    )

time: 2800 us -> 654 us (0.23)
  waiting for transfers between devices: 1860 us -> 0 us
  Pallas kernels: 0 us -> 469 us
  matrix products: 464 us -> 102 us
  local copies, waits for them, and re-layouts: 182 us -> 44.6 us
  other arithmetic: 158 us -> 32.7 us
  blocking collectives: 109 us -> 0 us
    reduce_scatter x8 -> x0, waiting for transfers between devices: 1390 us -> none  [the longest x1 361 us: on_device(): lax.psum_scatter(grad_up, ('dp', 'seq'), scatter_dimension=0, tiled=True)]
    pallas_call x0 -> x4, Pallas kernels: none -> 469 us  [the longest x3 237 us: hosted(): pl.pallas_call(kernel, grid=(steps,), out_shape=all_shape, in_specs=all_i...]
    dot_general x35 -> x0, matrix products: 317 us -> none  [the longest x7 67.5 us: rows_dot(): return jnp.dot(left_side, right_side, preferred_element_type=jnp.float32)]
    all_gather x9 -> x0, waiting for transfers between devices: 255 us -> none  [the longest x1 79 us: on_device(): self_keyval = lax.all_gather(keyval_local, 'seq', axis=1, tiled=True)]
    unnamed x21 -> x0, waiting for transfers between devices: 219 us -> none
    convert_element_type x23 -> x1, other arithmetic: 79.9 us -> 2.65 us  [half(): return values.astype(jnp.bfloat16)]
    all_gather x1 -> x0, blocking collectives: 65.8 us -> none  [on_device(): lax.all_gather(ffn_upbias, ('dp', 'seq'), axis=0, tiled=True)]
    dynamic_update_slice x28 -> x0, local copies, waits for them, and re-layouts: 54.8 us -> none  [the longest x14 23.3 us: on_device(): lax.map(cross_backward, (cross_queries, cross_kv, text_allowed, cross_log...]
  transfers between devices with their start and end apart: 19 -> 0, of which waited for: 15 -> 0; matrix products, arithmetic and copies ran while one was open for 22% -> 0% of each run, Pallas kernels for 0% -> 0%
where the time goes in v1:
time: 654 us; the launch traced here: 650 us
  Pallas kernels  469 us (72%)
  matrix products  102 us (16%)
  local copies, waits for them, and re-layouts  44.6 us (7%)
  other arithmetic  32.7 us (5%)
    pallas_call x3, Pallas kernels, hosted(): pl.pallas_call(kernel, grid=(steps,), out_shape=all_shape, in_specs=all_i...  237 us
    pallas_call x1, Pallas kernels, forward(): pl.pallas_call(functools.partial(forward_kernel, depth, sizes), out_shape...  232 us
    dot_general x7, matrix products, right_dot(): lax.dot_general(left_side, right_side, (((1,), (1,)), ((), ())), preferre...  54.6 us
    dot_general x7, matrix products, left_dot(): lax.dot_general(left_side, right_side, (((0,), (0,)), ((), ())), preferre...  47.1 us
    unnamed x137, local copies, waits for them, and re-layouts  17 us

profile of v1, /device:TPU:0, one launch (start us, length us, event | category | flops | bytes accessed | tf_op | source)
XLA Modules:
  0.0 649.7 jit_solution(10257004052678389481)
XLA Ops:
  0.8 1.7 fusion.19
  2.6 1.7 reshape.304
  4.5 1.8 reshape.305.refs_11_
  6.9 0.6 pad.8.refs_5_
  7.5 231.8 %forward.1 = (bf16[4,2,2,2,32,128]{5,4,3,2,1,0:T(8,128)(2,1)}, bf16[4,2,2,2,32,3072]{5,4,3,2,1,0:T(8,128)(2,1)}, bf16[4,2,2,2,32,1024]{5,4,3,2,1,0:T(8,128)(2,1)...) custom-call(bf16[2,512,1024]{2,1,0:T(8,128)(2,1)} %refs_0_.1, ...), custom_call_target="tpu_custom_call" | custom-call | tf_op jit(solution)/shard_map/forward/pallas_call | solution.py:1460
  239.3 17.2 %convert_reduce_fusion = (f32[4096]{0:T(1024)}, bf16[1024,4096]{1,0:T(8,128)(2,1)}) fusion(bf16[1024,4096]{1,0:T(8,128)(2,1)} %get-tuple-element.86, bf16[1024,1024]{1,0:T(8,128)(2,1)} %get-tuple-element.81, bf16[1024,1024]{1,0:T(8,128)(2,1)} %bitcast.181, bf16[1024,1024]{1,0:T(8,128)(2,1)} %bitcast.180, bf16[1024,1024]{1,0:T(8,128)(2,1)} %bitcast.179, ...), kind=kOutput, calls=%fused_computation | convolution fusion | flops 8644456448 | bytes 27279360 | tf_op jit(solution)/shard_map/dot_general | solution.py:41
  256.5 2.4 reduce_sum.218
  258.9 2.9 multiply_reduce_fusion.8
  261.8 0.8 fusion.20
  262.7 14.9 %multiply_reduce_fusion.1 = (f32[1024]{0:T(1024)S(1)}, f32[1024]{0:T(1024)S(1)}, f32[1024]{0:T(1024)S(1)}, f32[1024,1024]{1,0:T(8,128)S(1)}) fusion(f32[1024,1024]{1,0:T(8,128)S(1)} %copy-done.1, f32[1024]{0:T(1024)S(1)} %fusion.8, f32[1024]{0:T(1024)S(1)} %broadcast_multiply_fusion.2, f32[1024]{0:T(1024)S(1)} %bitcast.152, ...), kind=kOutput, calls=%fused_computation.18 | convolution fusion | flops 8598320128 | bytes 25190400 | tf_op jit(solution)/shard_map/dot_general | solution.py:41
  277.7 3.0 fusion.17
  280.6 2.4 reduce_sum.225
  283.1 5.5 convert_reduce_fusion.1
  288.6 3.7 convolution_convert_fusion.8.refs_5_
  292.4 11.3 %convolution_convert_fusion.1 = bf16[1024,4096]{1,0:T(8,128)(2,1)} fusion(bf16[1024,1024]{1,0:T(8,128)(2,1)S(1)} %copy-done.45, bf16[1024,4096]{1,0:T(8,128)(2,1)S(1)} %bitcast.183), kind=kOutput, calls=%fused_computation.10 | convolution fusion | flops 8594128896 | bytes 18874368 | tf_op jit(solution)/shard_map/dot_general | solution.py:35
  303.7 9.6 %convolution_convert_fusion = bf16[4096,1024]{1,0:T(8,128)(2,1)S(1)} fusion(bf16[1024,4096]{1,0:T(8,128)(2,1)S(1)} %bitcast.171, bf16[1024,1024]{1,0:T(8,128)(2,1)S(1)} %copy-done.44), kind=kOutput, calls=%fused_computation.9 | convolution fusion | flops 8594128896 | bytes 18874368 | tf_op jit(solution)/shard_map/dot_general | solution.py:35
  313.3 3.4 fusion.18
  316.8 0.6 dynamic_slice.3
  317.4 0.6 compare_select_fusion
  318.0 0.8 broadcast_in_dim.40.refs_3_
  318.8 105.8 %cross_attend_back.1 = (bf16[1024,1024]{1,0:T(8,128)(2,1)}, bf16[256,1024]{1,0:T(8,128)(2,1)}, bf16[256,1024]{1,0:T(8,128)(2,1)}, f32[32,4096]{1,0:T(8,128)}, f3...) custom-call(bf16[1024,1024]{1,0:T(8,128)(2,1)} %get-tuple-element.77, ...), custom_call_target="tpu_custom_call" | custom-call | tf_op jit(solution)/shard_map/cross_attend_back/pallas_call | solution.py:915
  424.6 1.9 pad_maximum_fusion
  426.5 1.1 constant_dynamic-update-slice_fusion.1
  427.6 1.2 constant_dynamic-update-slice_fusion
  428.9 2.2 convolution_convert_fusion.9
  431.1 3.8 convolution_convert_fusion.5
  434.9 3.7 convolution_convert_fusion.6
  438.6 3.4 convolution_convert_fusion.3
  442.0 0.9 copy-done.42
  442.8 2.8 multiply_reduce_fusion.2
  445.7 1.7 fusion.16
  447.4 0.5 copy-done.2
  447.9 1.3 copy-done.5
  449.2 1.2 convert_reduce_fusion.3
  450.8 3.7 convolution_convert_fusion.7.refs_4_
  454.5 59.4 %self_attend_back.1 = (bf16[1024,1024]{1,0:T(8,128)(2,1)}, bf16[1024,1024]{1,0:T(8,128)(2,1)}, bf16[1024,1024]{1,0:T(8,128)(2,1)}, f32[32,2048]{1,0:T(8,128)}, f...) custom-call(bf16[1024,3072]{1,0:T(8,128)(2,1)} %get-tuple-element.97.refs_0_.refs_1_.refs_2_, ...), custom_call_target="tpu_custom_call" | custom-call | tf_op jit(solution)/shard_map/self_attend_back/pallas_call | solution.py:915
  513.9 1.9 constant_dynamic-update-slice_fusion.4
  516.3 0.5 copy-done.6
  516.9 0.9 copy-done.3
  518.2 10.1 %multiply_reduce_fusion = (f32[1024]{0:T(1024)S(1)}, f32[1024,1024]{1,0:T(8,128)S(1)}) fusion(bf16[2,512,1024]{2,1,0:T(8,128)(2,1)S(1)} %copy-done.3, f32[1024]{0:T(1024)S(1)} %bitcast.147, f32[1024]{0:T(1024)S(1)} %bitcast.144, bf16[1024,3072]{1,0:T(8,128)(2,1)S(1)} %constant_dynamic-update-slice_fusion.2, bf16[1024,3072]{1,0:T(8,128)(2,1)} %bitcast.173), kind=kOutput, calls=%fused_computation.17 | convolution fusion | flops 6447692800 | bytes 18886656 | tf_op jit(solution)/shard_map/dot_general | solution.py:41
  528.3 0.7 multiply_reduce_fusion.4
  529.1 2.7 fusion.14
  531.8 2.6 add_convert_fusion
  534.6 2.0 convert_reduce_fusion.5
  537.3 2.1 convert_reduce_fusion.2
  539.9 0.9 slice_reduce_fusion
  541.4 0.9 pad.9.clone
  542.3 6.5 convolution_convert_fusion.4
  548.8 8.8 %convolution_convert_fusion.2 = bf16[1024,3072]{1,0:T(8,128)(2,1)} fusion(bf16[1024,1024]{1,0:T(8,128)(2,1)S(1)} %copy-done.40, bf16[1024,3072]{1,0:T(8,128)(2,1)S(1)} %bitcast.141), kind=kOutput, calls=%fused_computation.14 | convolution fusion | flops 6445596672 | bytes 14680064 | tf_op jit(solution)/shard_map/dot_general | solution.py:35
  557.6 72.0 %sum_last.1 = (f32[32,3072]{1,0:T(8,128)}, f32[32,1024]{1,0:T(8,128)}, f32[32,128]{1,0:T(8,128)}, bf16[2,512,1024]{2,1,0:T(8,128)(2,1)}) custom-call(bf16[4,2,2,2,32,3072]{5,4,3,2,1,0:T(8,128)(2,1)} %bitcast.132, bf16[4,2,2,2,32,1024]{5,4,3,2,1,0:T(8,128)(2,1)} %bitcast.134, f32[4,2,2,2,32,128]{5,4,3,2,1,0:T(8,128)} %bitcast.136, bf16[2,512,1024]{2,1,0:T(8,128)(2,1)} %bitcast.127), custom_call_target="tpu_custom_call" | custom-call | tf_op jit(solution)/shard_map/sum_last/pallas_call | solution.py:915
  629.5 1.6 slice_bitcast_fusion
  631.1 0.7 slice.100
  631.8 0.6 reshape.345
  632.4 0.7 reshape.343
  633.1 3.1 copy.61
  636.2 4.6 reshape.344
  640.7 3.2 copy.93
  643.9 1.3 copy.94
  645.3 0.8 copy.95
  646.0 0.7 copy.96
  646.8 0.7 copy.97
  647.5 0.7 copy.98
  648.1 0.7 copy.99
  648.8 0.7 copy.100
  (161 shorter events, 4.2 us)
Async XLA Ops:
  0.7 5.7 copy-start.47
  0.7 5.7 copy-start.24
  0.7 5.7 copy-start.25
  0.7 5.7 copy-start.34
  0.7 5.7 copy-start.35
  0.7 5.7 copy-start.36
  0.7 5.7 copy-start.37
  0.7 5.7 copy-start.38
  0.8 5.7 copy-start.26
  0.8 5.7 copy-start.27
  0.8 5.7 copy-start.28
  0.8 5.7 copy-start.29
  0.8 5.7 copy-start.30
  0.8 5.7 copy-start.31
  0.8 5.7 copy-start.32
  0.8 5.7 copy-start.33
  258.9 3.8 copy-start.1
  283.1 5.5 copy-start.46
  283.1 9.2 %slice-start.4 = ((s8[8388608]{0:T(1024)(128)(4,1)}), s8[4194304]{0:T(1024)(128)(4,1)S(1)}, s32[]{:S(2)}) async-start(s8[8388608]{0:T(1024)(128)(4,1)} %bitcast.182), calls=%async_computation.4 | async-start | bytes 8388608
  288.6 3.7 copy-start.45
  288.6 3.7 slice-start.5
  288.6 15.1 %slice-start.2 = ((s8[8388608]{0:T(1024)(128)(4,1)}), s8[4194304]{0:T(1024)(128)(4,1)S(1)}, s32[]{:S(2)}) async-start(s8[8388608]{0:T(1024)(128)(4,1)} %bitcast.170), calls=%async_computation.2 | async-start | bytes 8388608
  292.3 11.4 %slice-start.3 = ((s8[8388608]{0:T(1024)(128)(4,1)}), s8[4194304]{0:T(1024)(128)(4,1)S(1)}, s32[]{:S(2)}) async-start(s8[8388608]{0:T(1024)(128)(4,1)} %bitcast.170), calls=%async_computation.3 | async-start | bytes 8388608
  292.3 11.4 %copy-start.44 = (bf16[1024,1024]{1,0:T(8,128)(2,1)S(1)}, bf16[1024,1024]{1,0:T(8,128)(2,1)}, u32[]{:S(2)}) copy-start(bf16[1024,1024]{1,0:T(8,128)(2,1)} %get-tuple-element.81) | copy-start | bytes 6291460
  313.3 3.5 copy-start.23
  318.8 110.1 %copy-start.39 = (bf16[4,2,2,2,32,2048]{5,4,3,2,1,0:T(8,128)(2,1)S(1)}, bf16[4,2,2,2,32,2048]{5,4,3,2,1,0:T(8,128)(2,1)}, u32[]{:S(2)}) copy-start(bf16[4,2,2,2,32,2048]{5,4,3,2,1,0:T(8,128)(2,1)} %get-tuple-element.108) | copy-start | bytes 12582916
  427.6 3.5 copy-start.11
  431.1 3.8 copy-start.7
  431.1 3.8 copy-start.43
  434.9 3.8 copy-start.13
  438.6 3.4 copy-start
  438.6 4.2 copy-start.42
  445.7 2.2 copy-start.2
  445.7 3.5 copy-start.5
  449.2 1.6 copy-start.41
  450.4 81.4 %copy-start.4 = (f32[1024,1024]{1,0:T(8,128)}, f32[1024,1024]{1,0:T(8,128)S(1)}, u32[]{:S(2)}) copy-start(f32[1024,1024]{1,0:T(8,128)S(1)} %get-tuple-element.143) | copy-start | bytes 12582916
  513.9 2.2 copy-start.9
  513.9 2.8 copy-start.6
  516.1 1.7 copy-start.3
  516.9 11.4 %copy-start.14 = (bf16[1024,3072]{1,0:T(8,128)(2,1)}, bf16[1024,3072]{1,0:T(8,128)(2,1)S(1)}, u32[]{:S(2)}) copy-start(bf16[1024,3072]{1,0:T(8,128)(2,1)S(1)} %constant_dynamic-update-slice_fusion.2) | copy-start | bytes 18874372
  534.4 5.1 copy-start.10
  534.4 6.7 %copy-start.22 = (f32[4096]{0:T(1024)S(1)}, f32[4096]{0:T(1024)}, u32[]{:S(2)}) copy-start(f32[4096]{0:T(1024)} %get-tuple-element.182) | copy-start | bytes 49156
  537.0 5.2 copy-start.12
  541.4 7.4 %slice-start = ((s8[6291456]{0:T(1024)(128)(4,1)}), s8[4194304]{0:T(1024)(128)(4,1)S(1)}, s32[]{:S(2)}) async-start(s8[6291456]{0:T(1024)(128)(4,1)} %bitcast.140), calls=%async_computation | async-start | bytes 8388608
  542.3 6.5 slice-start.1
  542.3 6.5 copy-start.40
  557.6 74.8 %copy-start.15 = (f32[32,4096]{1,0:T(8,128)S(1)}, f32[32,4096]{1,0:T(8,128)}, u32[]{:S(2)}) copy-start(f32[32,4096]{1,0:T(8,128)} %get-tuple-element.123) | copy-start | bytes 1572868
  636.2 7.7 %copy-start.8 = (bf16[2,512,1024]{2,1,0:T(8,128)(2,1)S(1)}, bf16[2,512,1024]{2,1,0:T(8,128)(2,1)}, u32[]{:S(2)}) copy-start(bf16[2,512,1024]{2,1,0:T(8,128)(2,1)} %get-tuple-element.212) | copy-start | bytes 6291460
  640.7 4.5 copy-start.16
  640.7 5.3 copy-start.17
  640.7 6.1 copy-start.21
  643.9 3.5 copy-start.20
  643.9 4.2 copy-start.18
  643.9 4.9 copy-start.19
